TPU v7x, 256 devices: a whole 4x4x8 slice. The times are simulated.
256 devices in a mesh: dp: 16 (over y, z_lo, core), patch: 16 (over z_hi, x).
Axes of the slice: x: 4, y: 4, z: 8 (z_hi: 4, z_lo: 2; z = z_hi * 2 + z_lo), core: 2. Of those that a mesh axis runs over, the one named last changes fastest.
Arguments:
- patch_queries: bfloat16 [16, 4096, 512], P('dp', 'patch'), may hold values from -6 to 6
- patch_keys: bfloat16 [16, 4096, 512], P('dp', 'patch'), may hold values from -6 to 6
- patch_values: bfloat16 [16, 4096, 512], P('dp', 'patch'), may hold values from -6 to 6
- residual: float32 [16, 4096, 1024], P('dp', 'patch'), may hold values from -2 to 2
- teacher: bfloat16 [16, 4096, 1024], P('dp', 'patch'), may hold values from -6 to 6
- output_weight: bfloat16 [512, 1024], replicated, may hold values from -0.25 to 0.25
Outputs:
- d_queries: float32 [16, 4096, 512], P('dp', 'patch')
- d_keys: float32 [16, 4096, 512], P('dp', 'patch')
- d_values: float32 [16, 4096, 512], P('dp', 'patch')
- d_features: float32 [16, 4096, 1024], P('dp', 'patch')
- d_output_weight: float32 [512, 1024], replicated
All inputs are finite; a program needn't handle non-finite values.
Results may differ from a plain program's by a relative error of at most 0.017.
Values may be sent and summed in bfloat16 or wider, within the bound.
A program may use at most 128 MiB of HBM per device.

v0:
```python
import jax
import jax.numpy as jnp
from jax import lax
from jax.sharding import PartitionSpec as P

HEADS = 8
HEAD = 64
ROUNDS = 3


def passed_along(block, axis, distance):
    devices = range(lax.axis_size(axis))
    route = [((i - distance) % len(devices), i) for i in devices]
    return lax.ppermute(block, axis, route)


def gram_tile(left_student, left_teacher, right_student, right_teacher):
    first = jnp.einsum("ad,bd->ab", left_student, right_student, preferred_element_type=jnp.float32)
    second = jnp.einsum(
        "ad,bd->ab", left_teacher, right_teacher, preferred_element_type=jnp.float32
    )
    return (first - second).astype(jnp.bfloat16)


def transposed_term(tile_rounded, own_student):
    return jnp.einsum("ab,ad->bd", tile_rounded, own_student, preferred_element_type=jnp.float32)


def on_device(patch_queries, patch_keys, patch_values, residual, teacher, output_weight):
    queries = patch_queries[0]
    own_keys = patch_keys[0]
    own_values = patch_values[0]
    row_count = queries.shape[0]
    width = HEADS * HEAD
    score_scale = HEAD ** (-0.5)
    all_keys, all_values = (
        lax.all_gather(own_keys, "patch", axis=0, tiled=True),
        lax.all_gather(own_values, "patch", axis=0, tiled=True),
    )
    key_total = all_keys.shape[0]
    key_block = min(512, key_total)
    block_count = key_total // key_block
    key_blocks = all_keys.reshape(block_count, key_block, HEADS, HEAD)
    value_blocks = all_values.reshape(block_count, key_block, HEADS, HEAD)
    query_heads = queries.reshape(row_count, HEADS, HEAD)

    def forward_block(carry, pieces):
        running_max, running_total, weighted = carry
        block_keys, block_values = pieces
        scores = (
            jnp.einsum("qhd,khd->hqk", query_heads, block_keys, preferred_element_type=jnp.float32)
            * score_scale
        )
        new_max = jnp.maximum(running_max, jnp.max(scores, axis=2))
        rescale = jnp.exp(running_max - new_max)
        expo = jnp.exp(scores - new_max[:, :, None])
        running_total = running_total * rescale + jnp.sum(expo, axis=2)
        weighted = weighted * rescale[:, :, None] + jnp.einsum(
            "hqk,khd->hqd",
            expo.astype(jnp.bfloat16),
            block_values,
            preferred_element_type=jnp.float32,
        )
        return ((new_max, running_total, weighted), None)

    start_state = (
        jnp.full((HEADS, row_count), -1e30, jnp.float32),
        jnp.zeros((HEADS, row_count), jnp.float32),
        jnp.zeros((HEADS, row_count, HEAD), jnp.float32),
    )
    (row_max, row_total, weighted), unused = lax.scan(
        forward_block, start_state, (key_blocks, value_blocks)
    )
    log_total = row_max + jnp.log(row_total)
    attended = (
        (weighted / row_total[:, :, None])
        .transpose(1, 0, 2)
        .reshape(row_count, width)
        .astype(jnp.bfloat16)
    )
    features = residual[0] + jnp.dot(attended, output_weight, preferred_element_type=jnp.float32)
    inverse = lax.rsqrt(jnp.sum(features * features, axis=1, keepdims=True) + 1e-06)
    student = features * inverse
    student_rounded = student.astype(jnp.bfloat16)
    teacher_full = teacher[0].astype(jnp.float32)
    teacher_rounded = (
        teacher_full
        * lax.rsqrt(jnp.sum(teacher_full * teacher_full, axis=1, keepdims=True) + 1e-06)
    ).astype(jnp.bfloat16)
    own_tile = gram_tile(student_rounded, teacher_rounded, student_rounded, teacher_rounded)
    gradient = jnp.dot(own_tile, student_rounded, preferred_element_type=jnp.float32)
    for distance in range(1, ROUNDS + 1):
        lower_student, lower_teacher = passed_along(
            (student_rounded, teacher_rounded), "patch", distance
        )
        tile_rounded = gram_tile(student_rounded, teacher_rounded, lower_student, lower_teacher)
        gradient = gradient + jnp.dot(
            tile_rounded, lower_student, preferred_element_type=jnp.float32
        )
        returned = passed_along(
            transposed_term(tile_rounded, student_rounded).astype(jnp.bfloat16), "patch", -distance
        ).astype(jnp.float32)
        gradient = gradient + returned
    gram_grad = 32.0 * gradient
    d_features = inverse * (
        gram_grad - student * jnp.sum(student * gram_grad, axis=1, keepdims=True)
    )
    features_grad_rounded = d_features.astype(jnp.bfloat16)
    d_attended = jnp.einsum(
        "qd,hd->qh", features_grad_rounded, output_weight, preferred_element_type=jnp.float32
    ).astype(jnp.bfloat16)
    weight_term = jnp.einsum(
        "qh,qd->hd", attended, features_grad_rounded, preferred_element_type=jnp.float32
    )
    d_output_weight = lax.psum(weight_term, ("dp", "patch"))
    row_dot = jnp.sum(
        (d_attended.astype(jnp.float32) * attended.astype(jnp.float32)).reshape(
            row_count, HEADS, HEAD
        ),
        axis=2,
    ).T
    grad_heads = d_attended.reshape(row_count, HEADS, HEAD)

    def backward_block(query_grad, pieces):
        block_keys, block_values = pieces
        scores = (
            jnp.einsum("qhd,khd->hqk", query_heads, block_keys, preferred_element_type=jnp.float32)
            * score_scale
        )
        prob_exact = jnp.exp(scores - log_total[:, :, None])
        prob_weights = prob_exact.astype(jnp.bfloat16)
        prob_grad = jnp.einsum(
            "qhd,khd->hqk", grad_heads, block_values, preferred_element_type=jnp.float32
        )
        score_grad = (prob_exact * (prob_grad - row_dot[:, :, None])).astype(jnp.bfloat16)
        query_grad = query_grad + score_scale * jnp.einsum(
            "hqk,khd->hqd", score_grad, block_keys, preferred_element_type=jnp.float32
        )
        key_term = (
            score_scale
            * jnp.einsum(
                "hqk,qhd->khd", score_grad, query_heads, preferred_element_type=jnp.float32
            )
        ).astype(jnp.bfloat16)
        value_term = jnp.einsum(
            "hqk,qhd->khd", prob_weights, grad_heads, preferred_element_type=jnp.float32
        ).astype(jnp.bfloat16)
        joined = jnp.concatenate(
            [key_term.reshape(key_block, width), value_term.reshape(key_block, width)], axis=1
        )
        return (query_grad, joined)

    query_grad, joined_terms = lax.scan(
        backward_block, jnp.zeros((HEADS, row_count, HEAD), jnp.float32), (key_blocks, value_blocks)
    )
    joined_terms = joined_terms.reshape(key_total, 2 * width)
    summed = lax.psum_scatter(
        joined_terms.astype(jnp.float32).astype(jnp.bfloat16),
        "patch",
        scatter_dimension=0,
        tiled=True,
    ).astype(jnp.float32)
    d_queries = query_grad.transpose(1, 0, 2).reshape(row_count, width)
    return (
        d_queries[None],
        summed[:, :width][None],
        summed[:, width:][None],
        d_features[None],
        d_output_weight,
    )


def solution(mesh):
    placed = (
        P("dp", "patch", None),
        P("dp", "patch", None),
        P("dp", "patch", None),
        P("dp", "patch", None),
        P("dp", "patch", None),
        P(),
    )
    return jax.shard_map(
        on_device,
        mesh=mesh,
        in_specs=placed,
        out_specs=(
            P("dp", "patch", None),
            P("dp", "patch", None),
            P("dp", "patch", None),
            P("dp", "patch", None),
            P(),
        ),
        check_vma=False,
    )
```

profile of v0, /device:TPU:2, one launch (start us, length us, event | category | flops | bytes accessed | tf_op | source)
XLA Modules:
  0.0 917.0 jit_solution(18046005480120873436)
XLA Ops:
  19.8 19.4 %collective-permute-done.7 = bf16[256,1024]{1,0:T(8,128)(2,1)} collective-permute-done((bf16[256,1024]{1,0:T(8,128)(2,1)S(1)}, bf16[256,1024]{1,0:T(8,128)(2,1)}, u32[]{:S(2)}, u32[]{:S(2)}) %collective-permute-start.7) | collective-permute-done | bytes 524320 | tf_op jit(solution)/shard_map/ppermute | solution.py:14
  41.2 16.3 %collective-permute-done.4 = bf16[256,1024]{1,0:T(8,128)(2,1)S(1)} collective-permute-done((bf16[256,1024]{1,0:T(8,128)(2,1)S(1)}, bf16[256,1024]{1,0:T(8,128)(2,1)S(1)}, u32[]{:S(2)}, u32[]{:S(2)}) %collective-permute-start.4) | collective-permute-done | bytes 524320 | tf_op jit(solution)/shard_map/ppermute | solution.py:14
  59.7 51.3 %all-gather.5.cloned.1.call-done = bf16[1,4096,512]{2,1,0:T(8,128)(2,1)} async-done(((bf16[1,256,512]{2,1,0:T(8,128)(2,1)}), bf16[1,4096,512]{2,1,0:T(8,128)(2,1)}) %all-gather.5.cloned.1.call-update) | async-done | bytes 4194320 | tf_op jit(solution)/shard_map/all_gather | solution.py:37
  111.0 11.2 %reshape.81 = bf16[8,512,8,64]{3,2,1,0:T(8,128)(2,1)} reshape(bf16[1,4096,512]{2,1,0:T(8,128)(2,1)} %all-gather.5.cloned.1.call-done) | data formatting | bytes 8388608 | tf_op jit(solution)/shard_map/reshape | solution.py:43
  122.2 9.7 %copy.26 = bf16[8,512,8,64]{1,3,2,0:T(8,128)(2,1)} copy(bf16[8,512,8,64]{3,2,1,0:T(8,128)(2,1)} %reshape.81) | data formatting | bytes 8388608
  131.9 75.5 %all-gather.7.cloned.1.call-done = bf16[1,4096,512]{2,1,0:T(8,128)(2,1)} async-done(((bf16[1,256,512]{2,1,0:T(8,128)(2,1)}), bf16[1,4096,512]{2,1,0:T(8,128)(2,1)}) %all-gather.7.cloned.1.call-update) | async-done | bytes 4194320 | tf_op jit(solution)/shard_map/all_gather | solution.py:38
  207.4 11.2 %reshape.82 = bf16[8,512,8,64]{3,2,1,0:T(8,128)(2,1)} reshape(bf16[1,4096,512]{2,1,0:T(8,128)(2,1)} %all-gather.7.cloned.1.call-done) | data formatting | bytes 8388608 | tf_op jit(solution)/shard_map/reshape | solution.py:44
  218.6 9.8 %copy.22 = bf16[8,512,8,64]{1,3,2,0:T(8,128)(2,1)} copy(bf16[8,512,8,64]{3,2,1,0:T(8,128)(2,1)} %reshape.82) | data formatting | bytes 8388608
  228.4 73.8 %while.28 = (s32[]{:T(128)}, f32[8,256]{1,0:T(8,128)S(1)}, f32[8,256]{1,0:T(8,128)S(1)}, f32[8,256,64]{1,2,0:T(8,128)S(1)}, bf16[8,512,8,64]{1,3,2,0:T(8,128)(2,...) while((s32[]{:T(128)}, f32[8,256]{1,0:T(8,128)S(1)}, ...), condition=%wide.region_3.4_spmd.clone, body=%wide.region_0.3_spmd.clone.sunk | while | flops 277227520 | bytes 31850644 | solution.py:71
  228.4 3.8 bitcast_reduce_fusion.3
  246.9 3.8 bitcast_reduce_fusion.3
  256.1 3.8 bitcast_reduce_fusion.3
  265.3 3.8 bitcast_reduce_fusion.3
  274.5 3.8 bitcast_reduce_fusion.3
  283.8 3.8 bitcast_reduce_fusion.3
  293.0 3.8 bitcast_reduce_fusion.3
  304.4 4.0 collective-permute-start.6
  318.1 17.1 %collective-permute-done.6 = bf16[256,1024]{1,0:T(8,128)(2,1)} collective-permute-done((bf16[256,1024]{1,0:T(8,128)(2,1)S(1)}, bf16[256,1024]{1,0:T(8,128)(2,1)}, u32[]{:S(2)}, u32[]{:S(2)}) %collective-permute-start.6) | collective-permute-done | bytes 524320 | tf_op jit(solution)/shard_map/ppermute | solution.py:14
  340.5 20.7 %collective-permute-done.3 = bf16[256,1024]{1,0:T(8,128)(2,1)} collective-permute-done((bf16[256,1024]{1,0:T(8,128)(2,1)S(1)}, bf16[256,1024]{1,0:T(8,128)(2,1)}, u32[]{:S(2)}, u32[]{:S(2)}) %collective-permute-start.3) | collective-permute-done | bytes 524320 | tf_op jit(solution)/shard_map/ppermute | solution.py:14
  364.8 19.7 %collective-permute-start.2 = (bf16[256,1024]{1,0:T(8,128)(2,1)S(1)}, bf16[256,1024]{1,0:T(8,128)(2,1)S(1)}, u32[]{:S(2)}, u32[]{:S(2)}) collective-permute-start(bf16[256,1024]{1,0:T(8,128)(2,1)S(1)} %convolution_convert_fusion.2), channel_id=1, source_target_pairs={{1,0},{2,1},{3,2},{4,3},{5,4},{6,5},{7,6},{8,7},{9,8},{10,9},{11,1... | collective-permute-start | bytes 1572872 | tf_op jit(solution)/shard_map/ppermute | solution.py:14
  387.2 7.1 collective-permute-done.2
  399.0 111.6 %while.29 = (s32[]{:T(128)}, f32[8,256,64]{1,2,0:T(8,128)}, bf16[8,512,1024]{2,1,0:T(8,128)(2,1)}, bf16[8,512,8,64]{1,3,2,0:T(8,128)(2,1)}, bf16[256,8,64]{0,2,1...) while((s32[]{:T(128)}, f32[8,256,64]{1,2,0:T(8,128)}, ...), condition=%wide.region_9.10_spmd.clone, body=%wide.region_8.9_spmd.clone.sunk | while | flops 682754048 | bytes 50880740 | solution.py:153
  514.7 126.7 %reduce-scatter.2.cloned.1.call-done = bf16[256,1024]{1,0:T(8,128)(2,1)} async-done(((bf16[4096,1024]{1,0:T(8,128)(2,1)}), bf16[256,1024]{1,0:T(8,128)(2,1)}) %reduce-scatter.2.cloned.1.call-update) | async-done | bytes 524304 | tf_op jit(solution)/shard_map/reduce_scatter | solution.py:157
  643.6 263.7 %all-reduce.2.cloned.1.call-done = f32[512,1024]{1,0:T(8,128)} async-done(((f32[512,1024]{1,0:T(8,128)}), f32[512,1024]{1,0:T(8,128)}) %all-reduce.2.cloned.1.call-update) | async-done | bytes 2097168 | tf_op jit(solution)/shard_map/psum | solution.py:115
  (249 shorter events, 212.1 us)
Async XLA Ops:
  7.2 295.1 %copy-start = (bf16[512,1024]{1,0:T(8,128)(2,1)S(1)}, bf16[512,1024]{1,0:T(8,128)(2,1)}, u32[]{:S(2)}) copy-start(bf16[512,1024]{1,0:T(8,128)(2,1)} %param.15) | copy-start | bytes 3145732
  7.2 103.8 %all-gather.5.cloned.1.call-start = ((), (), s32[]{:S(2)}) async-start(), calls=%async_computation.3 | async-start | bytes 4456448 | tf_op jit(solution)/shard_map/all_gather | solution.py:37
  7.9 199.5 %all-gather.7.cloned.1.call-start = ((), (), s32[]{:S(2)}) async-start(), calls=%async_computation.4 | async-start | bytes 4456448 | tf_op jit(solution)/shard_map/all_gather | solution.py:38
  8.7 632.7 %reduce-scatter.2.cloned.1.call-start = ((), (), s32[]{:S(2)}) async-start(), calls=%async_computation.1 | async-start | bytes 8912896 | tf_op jit(solution)/shard_map/reduce_scatter | solution.py:157
  11.1 28.0 %collective-permute-start.7 = (bf16[256,1024]{1,0:T(8,128)(2,1)S(1)}, bf16[256,1024]{1,0:T(8,128)(2,1)}, u32[]{:S(2)}, u32[]{:S(2)}) collective-permute-start(bf16[256,1024]{1,0:T(8,128)(2,1)S(1)} %fusion.54), channel_id=1, source_target_pairs={{13,0},{14,1},{15,2},{0,3},{1,4},{2,5},{3,6},{4,7},{5,8},{6,9},{7,... | collective-permute-start | bytes 1572872 | tf_op jit(solution)/shard_map/ppermute | solution.py:14
  14.5 43.1 %collective-permute-start.4 = (bf16[256,1024]{1,0:T(8,128)(2,1)S(1)}, bf16[256,1024]{1,0:T(8,128)(2,1)S(1)}, u32[]{:S(2)}, u32[]{:S(2)}) collective-permute-start(bf16[256,1024]{1,0:T(8,128)(2,1)S(1)} %fusion.54), channel_id=1, source_target_pairs={{14,0},{15,1},{0,2},{1,3},{2,4},{3,5},{4,6},{5,7},{6,8},{7,9},{8,1... | collective-permute-start | bytes 1572872 | tf_op jit(solution)/shard_map/ppermute | solution.py:14
  16.9 41.7 %collective-permute-start.1 = (bf16[256,1024]{1,0:T(8,128)(2,1)S(1)}, bf16[256,1024]{1,0:T(8,128)(2,1)S(1)}, u32[]{:S(2)}, u32[]{:S(2)}) collective-permute-start(bf16[256,1024]{1,0:T(8,128)(2,1)S(1)} %fusion.54), channel_id=1, source_target_pairs={{15,0},{0,1},{1,2},{2,3},{3,4},{4,5},{5,6},{6,7},{7,8},{8,9},{9,10... | collective-permute-start | bytes 1572872 | tf_op jit(solution)/shard_map/ppermute | solution.py:14
  302.2 13.2 %copy-start.9 = (bf16[1,256,1024]{2,1,0:T(8,128)(2,1)S(1)}, bf16[1,256,1024]{2,1,0:T(8,128)(2,1)}, u32[]{:S(2)}) copy-start(bf16[1,256,1024]{2,1,0:T(8,128)(2,1)} %param.14) | copy-start | bytes 1572868
  304.4 30.9 %collective-permute-start.6 = (bf16[256,1024]{1,0:T(8,128)(2,1)S(1)}, bf16[256,1024]{1,0:T(8,128)(2,1)}, u32[]{:S(2)}, u32[]{:S(2)}) collective-permute-start(bf16[256,1024]{1,0:T(8,128)(2,1)S(1)} %multiply_convert_fusion.1), channel_id=1, source_target_pairs={{13,0},{14,1},{15,2},{0,3},{1,4},{2,5},{3,6},{4,7},{5,8},{6,9},{7,... | collective-permute-start | bytes 1572872 | tf_op jit(solution)/shard_map/ppermute | solution.py:14
  311.2 50.0 %collective-permute-start.3 = (bf16[256,1024]{1,0:T(8,128)(2,1)S(1)}, bf16[256,1024]{1,0:T(8,128)(2,1)}, u32[]{:S(2)}, u32[]{:S(2)}) collective-permute-start(bf16[256,1024]{1,0:T(8,128)(2,1)S(1)} %multiply_convert_fusion.1), channel_id=1, source_target_pairs={{14,0},{15,1},{0,2},{1,3},{2,4},{3,5},{4,6},{5,7},{6,8},{7,9},{8,1... | collective-permute-start | bytes 1572872 | tf_op jit(solution)/shard_map/ppermute | solution.py:14
  313.6 49.5 %collective-permute-start = (bf16[256,1024]{1,0:T(8,128)(2,1)S(1)}, bf16[256,1024]{1,0:T(8,128)(2,1)}, u32[]{:S(2)}, u32[]{:S(2)}) collective-permute-start(bf16[256,1024]{1,0:T(8,128)(2,1)S(1)} %multiply_convert_fusion.1), channel_id=1, source_target_pairs={{15,0},{0,1},{1,2},{2,3},{3,4},{4,5},{5,6},{6,7},{7,8},{8,9},{9,10... | collective-permute-start | bytes 1572872 | tf_op jit(solution)/shard_map/ppermute | solution.py:14
  318.1 44.9 %copy-start.14 = (f32[256,256]{1,0:T(8,128)S(1)}, f32[256,256]{1,0:T(8,128)}, u32[]{:S(2)}) copy-start(f32[256,256]{1,0:T(8,128)} %fusion.65) | copy-start | bytes 786436
  337.1 57.3 %copy-start.12 = (f32[256,1024]{1,0:T(8,128)S(1)}, f32[256,1024]{1,0:T(8,128)}, u32[]{:S(2)}) copy-start(f32[256,1024]{1,0:T(8,128)} %fusion.52) | copy-start | bytes 3145732
  337.1 50.2 %collective-permute-start.8 = (bf16[256,1024]{1,0:T(8,128)(2,1)S(1)}, bf16[256,1024]{1,0:T(8,128)(2,1)S(1)}, u32[]{:S(2)}, u32[]{:S(2)}) collective-permute-start(bf16[256,1024]{1,0:T(8,128)(2,1)S(1)} %convolution_convert_fusion), channel_id=1, source_target_pairs={{3,0},{4,1},{5,2},{6,3},{7,4},{8,5},{9,6},{10,7},{11,8},{12,9},{13... | collective-permute-start | bytes 1572872 | tf_op jit(solution)/shard_map/ppermute | solution.py:14
  363.0 24.3 %collective-permute-start.5 = (bf16[256,1024]{1,0:T(8,128)(2,1)S(1)}, bf16[256,1024]{1,0:T(8,128)(2,1)S(1)}, u32[]{:S(2)}, u32[]{:S(2)}) collective-permute-start(bf16[256,1024]{1,0:T(8,128)(2,1)S(1)} %convolution_convert_fusion.1), channel_id=1, source_target_pairs={{2,0},{3,1},{4,2},{5,3},{6,4},{7,5},{8,6},{9,7},{10,8},{11,9},{12,... | collective-permute-start | bytes 1572872 | tf_op jit(solution)/shard_map/ppermute | solution.py:14
  364.8 29.6 %collective-permute-start.2 = (bf16[256,1024]{1,0:T(8,128)(2,1)S(1)}, bf16[256,1024]{1,0:T(8,128)(2,1)S(1)}, u32[]{:S(2)}, u32[]{:S(2)}) collective-permute-start(bf16[256,1024]{1,0:T(8,128)(2,1)S(1)} %convolution_convert_fusion.2), channel_id=1, source_target_pairs={{1,0},{2,1},{3,2},{4,3},{5,4},{6,5},{7,6},{8,7},{9,8},{10,9},{11,1... | collective-permute-start | bytes 1572872 | tf_op jit(solution)/shard_map/ppermute | solution.py:14
  387.2 10.2 %copy-start.13 = (bf16[256,512]{1,0:T(8,128)(2,1)S(1)}, bf16[256,512]{1,0:T(8,128)(2,1)}, u32[]{:S(2)}) copy-start(bf16[256,512]{1,0:T(8,128)(2,1)} %copy.24) | copy-start | bytes 786436
  400.9 4.3 copy-start.4
  414.8 4.3 copy-start.4
  442.7 4.3 copy-start.4
  470.5 4.3 copy-start.4
  484.5 4.3 copy-start.4
  510.7 396.7 %all-reduce.2.cloned.1.call-start = ((), (), s32[]{:S(2)}) async-start(), calls=%async_computation.2 | async-start | bytes 4194304 | tf_op jit(solution)/shard_map/psum | solution.py:115
  513.7 396.8 %copy-start.1 = (bf16[512,1024]{1,0:T(8,128)(2,1)S(1)}, bf16[512,1024]{1,0:T(8,128)(2,1)}, u32[]{:S(2)}) copy-start(bf16[512,1024]{1,0:T(8,128)(2,1)} %param.15) | copy-start | bytes 3145732
  (32 other events, 71.0 us)
Sparse Core Ops, SparseCore 0:
  10.4 100.4 all-gather.4
  113.4 93.9 all-gather.6
  510.8 130.5 reduce-scatter.1
  647.2 260.0 all-reduce.1
where the time goes:
time: 920 us; the launch traced here: 917 us
  waiting for transfers between devices  599 us (65%)
  matrix products  144 us (16%)
  local copies, waits for them, and re-layouts  91.1 us (10%)
  starting transfers between devices  39.1 us (4%)
  other arithmetic  29 us (3%)
  between operations  14 us (2%)
    psum x1, waiting for transfers between devices, on_device(): d_output_weight = lax.psum(weight_term, ('dp', 'patch'))  264 us
    reduce_scatter x1, waiting for transfers between devices, on_device(): lax.psum_scatter(joined_terms.astype(jnp.float32).astype(jnp.bfloat16), '...  127 us
    ppermute x9, waiting for transfers between devices, passed_along(): return lax.ppermute(block, axis, route)  80.6 us
    all_gather x1, waiting for transfers between devices, on_device(): lax.all_gather(own_values, 'patch', axis=0, tiled=True)  75.5 us
    all_gather x1, waiting for transfers between devices, on_device(): lax.all_gather(own_keys, 'patch', axis=0, tiled=True)  51.3 us
    ppermute x9, starting transfers between devices, passed_along(): return lax.ppermute(block, axis, route)  39 us
    dot_general x8, matrix products, forward_block(): jnp.einsum('qhd,khd->hqk', query_heads, block_keys, preferred_element_typ...  30.2 us
    unnamed x27, local copies, waits for them, and re-layouts  26.9 us
  transfers between devices with their start and end apart: 13, of which 9 were waited for; matrix products, arithmetic and copies ran while one was open for 5% of the time, Pallas kernels for 0%

commit v1 on v0

v1 whole, which is shorter than its diff:
```python
import jax
import jax.numpy as jnp
from jax import lax
from jax.experimental import pallas as pl
from jax.experimental.pallas import tpu as pltpu
from jax.sharding import PartitionSpec as P

MESH = pl.DeviceIdType.MESH
F32 = jnp.float32
BF16 = jnp.bfloat16
ROWS = 256
PAIR = 128
HEAD = 64
OFFSETS = (0, 1, 3, 2)
VMEM_LIMIT = 60 * 1024 * 1024


def position():
    index = lax.axis_index("patch")
    return index // 4, index % 4


def on_patch(z, x):
    return {"patch": z * 4 + x}


def remote(src, dst, send_sem, recv_sem, device):
    return pltpu.make_async_remote_copy(
        src_ref=src,
        dst_ref=dst,
        send_sem=send_sem,
        recv_sem=recv_sem,
        device_id=device,
        device_id_type=MESH,
    )


def meet(peers):
    barrier = pltpu.get_barrier_semaphore()
    for peer in peers:
        pl.semaphore_signal(barrier, inc=1, device_id=peer, device_id_type=MESH)
    pl.semaphore_wait(barrier, len(peers))


def columns(index):
    return pl.ds(pl.multiple_of(index * PAIR, PAIR), PAIR)


def matmul(a, b):
    return jnp.dot(a, b, preferred_element_type=F32)


def matmul_t(a, b):
    return lax.dot_general(a, b, (((1,), (1,)), ((), ())), preferred_element_type=F32)


def head_lanes(rows):
    return lax.broadcasted_iota(jnp.int32, (rows, PAIR), 1) < HEAD


def normalised(block):
    return block * lax.rsqrt(jnp.sum(block * block, axis=1, keepdims=True) + 1e-06)


def forward_kernel(
    q_ref, k_ref, v_ref, t_ref,
    q2, kv, att_full, att2, fac, e_hbm, t_row, t_ud,
    e_buf, m_s, l_s, o_s,
    own_sem, zs, zr, xs, xr, rs, rr, tzs, tzr, txs, txr, trs, trr, as_, ar, a_own, e_sem,
):
    z, x = position()
    right, left, across = (x + 1) % 4, (x + 3) % 4, (x + 2) % 4
    up, down = (z + 1) % 4, (z + 3) % 4
    meet([on_patch((z + d) % 4, x) for d in (1, 2, 3)] + [on_patch(z, right), on_patch(z, left)])

    started = []

    def send(src, dst, send_sem, recv_sem, device):
        copy = remote(src, dst, send_sem, recv_sem, device)
        copy.start()
        started.append(copy)

    for d in (1, 3, 2):
        to = (z + d) % 4
        for i, source in enumerate((k_ref, v_ref)):
            send(source.at[:, columns(to)], kv.at[x, z, i], zs.at[i, d], zr.at[i, d], on_patch(to, x))
    own = [
        pltpu.make_async_copy(k_ref.at[:, columns(z)], kv.at[x, z, 0], own_sem.at[0]),
        pltpu.make_async_copy(v_ref.at[:, columns(z)], kv.at[x, z, 1], own_sem.at[1]),
        pltpu.make_async_copy(q_ref.at[:, columns(z)], q2.at[z], own_sem.at[2]),
    ]
    for copy in own:
        copy.start()
    for d in (1, 3, 2):
        to = (z + d) % 4
        send(q_ref.at[:, columns(to)], q2.at[z], zs.at[2, d], zr.at[2, d], on_patch(to, x))
    for copy in own:
        copy.wait()

    def spread(d):
        at = (z + 4 - d) % 4
        for side, to in enumerate((right, left)):
            send(kv.at[x, at], kv.at[x, at], xs.at[side, d], xr.at[side, d], on_patch(z, to))

    spread(0)
    t_row[x] = normalised(t_ref[...].astype(F32)).astype(BF16)
    for d in (1, 3, 2):
        at = (z + 4 - d) % 4
        for i in range(2):
            slot = kv.at[x, at, i]
            remote(slot, slot, zs.at[i, d], zr.at[i, d], on_patch(at, x)).wait_recv()
        spread(d)
    send(t_row.at[x], t_ud.at[0], tzs.at[0], tzr.at[0], on_patch(up, x))
    send(t_row.at[x], t_ud.at[1], tzs.at[1], tzr.at[1], on_patch(down, x))
    for d in (1, 2, 3):
        at = (z + 4 - d) % 4
        remote(q2.at[at], q2.at[at], zs.at[2, d], zr.at[2, d], on_patch(at, x)).wait_recv()

    first_head = head_lanes(ROWS)

    def chunk(c):
        xc = (x + OFFSETS[c]) % 4

        def block(qt, carry):
            keys = kv[xc, :, 0].reshape(1024, PAIR)
            values = kv[xc, :, 1].reshape(1024, PAIR)
            queries = q2[qt].astype(F32) * (HEAD ** -0.5)
            parts = []
            for h in range(2):
                mask = first_head if h == 0 else jnp.logical_not(first_head)
                masked = jnp.where(mask, queries, 0.0).astype(BF16)
                scores = matmul_t(masked, keys)
                top = jnp.max(scores, axis=1, keepdims=True)
                expo = jnp.exp(scores - top)
                total = jnp.sum(expo, axis=1, keepdims=True)
                rounded = expo.astype(BF16)
                e_buf[c, h, qt] = rounded
                parts.append((top, total, matmul(rounded, values)))
            (m0, l0, o0), (m1, l1, o1) = parts
            m_s[c, qt] = jnp.where(first_head, m0, m1)
            l_s[c, qt] = jnp.where(first_head, l0, l1)
            o_s[c, qt] = jnp.where(first_head, o0, o1)
            return carry

        lax.fori_loop(0, 4, block, 0)
        pltpu.make_async_copy(e_buf.at[c], e_hbm.at[c], e_sem.at[c]).start()

    def arrived(side, slot_x, d):
        at = (z + 4 - d) % 4
        slot = kv.at[slot_x, at]
        remote(slot, slot, xs.at[side, d], xr.at[side, d], on_patch(z, slot_x)).wait_recv()

    chunk(0)
    for d in (0, 1, 3, 2):
        at = (z + 4 - d) % 4
        arrived(1, right, d)
        send(kv.at[right, at, 0], kv.at[right, at, 0], rs.at[0, d], rr.at[0, d], on_patch(z, left))
        arrived(0, left, d)
        send(kv.at[left, at, 1], kv.at[left, at, 1], rs.at[1, d], rr.at[1, d], on_patch(z, right))
    for side, to in enumerate((right, left)):
        send(t_row.at[x], t_row.at[x], txs.at[side], txr.at[side], on_patch(z, to))
    chunk(1)
    chunk(2)
    half = ROWS // 2
    remote(t_row.at[right], t_row.at[right], txs.at[1], txr.at[1], on_patch(z, right)).wait_recv()
    upper = t_row.at[right, pl.ds(0, half)]
    send(upper, upper, trs.at[0], trr.at[0], on_patch(z, left))
    remote(t_row.at[left], t_row.at[left], txs.at[0], txr.at[0], on_patch(z, left)).wait_recv()
    lower = t_row.at[left, pl.ds(half, half)]
    send(lower, lower, trs.at[1], trr.at[1], on_patch(z, right))
    for d in range(4):
        at = (z + 4 - d) % 4
        for i in range(2):
            slot = kv.at[across, at, i]
            remote(slot, slot, rs.at[i, d], rr.at[i, d], on_patch(z, right)).wait_recv()
    chunk(3)

    for qt in range(4):
        top = jnp.maximum(
            jnp.maximum(m_s[0, qt], m_s[1, qt]), jnp.maximum(m_s[2, qt], m_s[3, qt])
        )
        scale = [jnp.exp(m_s[c, qt] - top) for c in range(4)]
        total = sum(scale[c] * l_s[c, qt] for c in range(4))
        joined = sum(scale[c] * o_s[c, qt] for c in range(4))
        inverse = 1.0 / total
        att2[qt] = (joined * inverse).astype(BF16)
        for c in range(4):
            fac[c, qt] = scale[c] * inverse
    for d in (1, 3, 2):
        to = (z + d) % 4
        send(att2.at[to], att_full.at[:, columns(z)], as_.at[d], ar.at[d], on_patch(to, x))
    own_att = pltpu.make_async_copy(att2.at[z], att_full.at[:, columns(z)], a_own)
    own_att.start()
    own_att.wait()
    for d in (1, 2, 3):
        at = (z + 4 - d) % 4
        remote(att2.at[at], att_full.at[:, columns(at)], as_.at[d], ar.at[d], on_patch(at, x)).wait_recv()
    for i in range(2):
        remote(t_ud.at[i], t_ud.at[i], tzs.at[i], tzr.at[i], on_patch(up, x)).wait_recv()
    upper, lower = t_row.at[across, pl.ds(0, half)], t_row.at[across, pl.ds(half, half)]
    remote(upper, upper, trs.at[0], trr.at[0], on_patch(z, right)).wait_recv()
    remote(lower, lower, trs.at[1], trr.at[1], on_patch(z, right)).wait_recv()
    for c in range(4):
        pltpu.make_async_copy(e_buf.at[c], e_hbm.at[c], e_sem.at[c]).wait()
    for copy in started:
        copy.wait_send()


def gram_kernel(
    att_ref, res_ref, w_ref, t_row, t_ud,
    d_features, datt2, w_term,
    s_row, s_ud, out_ud, in_ud, datt, student_s, inverse_s,
    szs, szr, sxs, sxr, srs, srr, bs, br, ds_, dr, d_own,
):
    z, x = position()
    right, left, across = (x + 1) % 4, (x + 3) % 4, (x + 2) % 4
    up, down = (z + 1) % 4, (z + 3) % 4
    half = ROWS // 2
    features = res_ref[...] + matmul(att_ref[...], w_ref[...])
    inverse = lax.rsqrt(jnp.sum(features * features, axis=1, keepdims=True) + 1e-06)
    student = features * inverse
    student_s[...] = student
    inverse_s[...] = jnp.broadcast_to(inverse, inverse_s.shape)
    s_row[x] = student.astype(BF16)
    meet([on_patch((z + d) % 4, x) for d in (1, 2, 3)] + [on_patch(z, right), on_patch(z, left)])

    started = []

    def send(src, dst, send_sem, recv_sem, device):
        copy = remote(src, dst, send_sem, recv_sem, device)
        copy.start()
        started.append(copy)

    send(s_row.at[x], s_ud.at[0], szs.at[0], szr.at[0], on_patch(up, x))
    send(s_row.at[x], s_ud.at[1], szs.at[1], szr.at[1], on_patch(down, x))
    for side, to in enumerate((right, left)):
        send(s_row.at[x], s_row.at[x], sxs.at[side], sxr.at[side], on_patch(z, to))

    remote(s_row.at[right], s_row.at[right], sxs.at[1], sxr.at[1], on_patch(z, right)).wait_recv()
    upper = s_row.at[right, pl.ds(0, half)]
    send(upper, upper, srs.at[0], srr.at[0], on_patch(z, left))
    remote(s_row.at[left], s_row.at[left], sxs.at[0], sxr.at[0], on_patch(z, left)).wait_recv()
    lower = s_row.at[left, pl.ds(half, half)]
    send(lower, lower, srs.at[1], srr.at[1], on_patch(z, right))
    upper, lower = s_row.at[across, pl.ds(0, half)], s_row.at[across, pl.ds(half, half)]
    remote(upper, upper, srs.at[0], srr.at[0], on_patch(z, right)).wait_recv()
    remote(lower, lower, srs.at[1], srr.at[1], on_patch(z, right)).wait_recv()

    def term(students, teachers, keep):
        row_students = s_row[...].reshape(1024, 1024)
        row_teachers = t_row[...].reshape(1024, 1024)
        tile = matmul_t(students, row_students) - matmul_t(teachers, row_teachers)
        if keep is not None:
            tile = jnp.where(keep(lax.broadcasted_iota(jnp.int32, tile.shape, 1)), tile, 0.0)
        return matmul(tile.astype(BF16), row_students)

    for i, to, keep in (
        (0, down, lambda column: column < x * ROWS),
        (1, up, lambda column: column >= (x + 1) * ROWS),
    ):
        remote(s_ud.at[i], s_ud.at[i], szs.at[i], szr.at[i], on_patch(to, x)).wait_recv()
        out_ud[i] = term(s_ud[i], t_ud[i], keep).astype(BF16)
        send(out_ud.at[i], in_ud.at[i], bs.at[i], br.at[i], on_patch(to, x))
    gradient = term(s_row[x], t_row[x], None)
    for i in range(2):
        remote(in_ud.at[i], in_ud.at[i], bs.at[i], br.at[i], on_patch(up, x)).wait_recv()
        gradient = gradient + in_ud[i].astype(F32)
    gram_grad = 32.0 * gradient
    student = student_s[...]
    inverse = inverse_s[:, :1]
    grad = inverse * (gram_grad - student * jnp.sum(student * gram_grad, axis=1, keepdims=True))
    d_features[...] = grad
    rounded = grad.astype(BF16)
    datt[...] = matmul_t(rounded, w_ref[...]).astype(BF16)
    for d in (1, 3, 2):
        to = (z + d) % 4
        send(datt.at[:, columns(to)], datt2.at[z], ds_.at[d], dr.at[d], on_patch(to, x))
    own = pltpu.make_async_copy(datt.at[:, columns(z)], datt2.at[z], d_own)
    own.start()
    transposed = att_ref[...].astype(F32).T.astype(BF16)
    w_term[...] = matmul(transposed, rounded).astype(BF16)
    own.wait()
    for d in (1, 2, 3):
        at = (z + 4 - d) % 4
        remote(datt2.at[at], datt2.at[at], ds_.at[d], dr.at[d], on_patch(at, x)).wait_recv()
    for copy in started:
        copy.wait_send()


def backward_kernel(
    q2, kv, att2, datt2, fac, w_term, e_hbm,
    d_queries, d_keys, d_values, d_weight,
    e_buf, q_t, dq_acc, dk_acc, dv_acc, do_t, part, rs_in, z_out, z_in, dq_out,
    ra, pa, rb, pb, rc, pc, gd, ge,
    e_sem, xs, xr, zs, zr, qs, qr,
    sa, da, sb, db, sc, dc, sd, dd, se, de,
):
    z, x = position()
    dp = lax.axis_index("dp")
    y, z_lo, core = dp // 4, (dp // 2) % 2, dp % 2
    near = y * 2 + core
    ring = z * 2 + z_lo

    def near_device(index):
        return {"dp": (index // 2) * 4 + z_lo * 2 + index % 2}

    def ring_device(index):
        return {"dp": y * 4 + (index % 2) * 2 + core, "patch": (index // 2) * 4 + x}

    for c in (3, 1, 2, 0):
        pltpu.make_async_copy(e_hbm.at[c], e_buf.at[c], e_sem.at[c]).start()
    meet(
        [ring_device((ring + d) % 8) for d in range(1, 8)]
        + [on_patch(z, (x + d) % 4) for d in range(1, 4)]
        + [near_device((near + d) % 8) for d in range(1, 8)]
    )
    started = []

    def send(src, dst, send_sem, recv_sem, device):
        copy = remote(src, dst, send_sem, recv_sem, device)
        copy.start()
        started.append(copy)

    def weight_a():
        for d in range(1, 8):
            to = (near + d) % 8
            send(w_term.at[pl.ds(pl.multiple_of(to * 64, 64), 64)], ra.at[d - 1], sa.at[d], da.at[d], near_device(to))

    def weight_b():
        total = w_term[pl.ds(pl.multiple_of(near * 64, 64), 64)].astype(F32)
        for d in range(1, 8):
            slot = ra.at[d - 1]
            remote(slot, slot, sa.at[d], da.at[d], near_device((near + d) % 8)).wait_recv()
            total = total + slot[...].astype(F32)
        pa[...] = total.astype(BF16)
        for d in range(1, 4):
            to = (x + d) % 4
            send(pa.at[pl.ds(pl.multiple_of(to * 16, 16), 16)], rb.at[d - 1], sb.at[d], db.at[d], on_patch(z, to))

    def weight_c():
        total = pa[pl.ds(pl.multiple_of(x * 16, 16), 16)].astype(F32)
        for d in range(1, 4):
            slot = rb.at[d - 1]
            remote(slot, slot, sb.at[d], db.at[d], on_patch(z, (x + d) % 4)).wait_recv()
            total = total + slot[...].astype(F32)
        pb[...] = total.astype(BF16)
        rc[ring] = pb[...]
        for d in range(1, 8):
            send(pb, rc.at[ring], sc.at[d], dc.at[d], ring_device((ring + d) % 8))

    def weight_d():
        for d in range(1, 8):
            at = (ring + 8 - d) % 8
            remote(rc.at[at], rc.at[at], sc.at[d], dc.at[d], ring_device(at)).wait_recv()
        total = rc[0].astype(F32)
        for i in range(1, 8):
            total = total + rc[i].astype(F32)
        pc[...] = total.astype(BF16)
        gd[x] = pc[...]
        for d in range(1, 4):
            send(pc, gd.at[x], sd.at[d], dd.at[d], on_patch(z, (x + d) % 4))

    def weight_e():
        for d in range(1, 4):
            at = (x + 4 - d) % 4
            remote(gd.at[at], gd.at[at], sd.at[d], dd.at[d], on_patch(z, at)).wait_recv()
        ge[near] = gd[...]
        for d in range(1, 8):
            send(gd, ge.at[near], se.at[d], de.at[d], near_device((near + d) % 8))

    def weight_out():
        for d in range(1, 8):
            at = (near + 8 - d) % 8
            remote(ge.at[at], ge.at[at], se.at[d], de.at[d], near_device(at)).wait_recv()
        d_weight[...] = ge[...].reshape(512, 1024).astype(F32)

    weight_a()
    first_head = head_lanes(ROWS)
    for qt in range(4):
        q_t[qt] = (q2[qt].astype(F32) * (HEAD ** -0.5)).T.astype(BF16)
        dq_acc[qt] = jnp.zeros((ROWS, PAIR), F32)

    def chunk(c):
        xc = (x + OFFSETS[c]) % 4
        pltpu.make_async_copy(e_hbm.at[c], e_buf.at[c], e_sem.at[c]).wait()
        dk_acc[...] = jnp.zeros_like(dk_acc)
        dv_acc[...] = jnp.zeros_like(dv_acc)

        def block(qt, carry):
            keys = kv[xc, :, 0].reshape(1024, PAIR)
            values = kv[xc, :, 1].reshape(1024, PAIR)
            factor = fac[c, qt]
            grads = datt2[qt].astype(F32)
            scaled = grads * factor
            do_t[...] = scaled.T.astype(BF16)
            dots = grads * att2[qt].astype(F32)
            found = []
            for h in range(2):
                mask = first_head if h == 0 else jnp.logical_not(first_head)
                rows = pl.ds(h * HEAD, HEAD)
                masked = jnp.where(mask, scaled, 0.0).astype(BF16)
                row_dot = jnp.sum(jnp.where(mask, dots, 0.0), axis=1, keepdims=True)
                row_dot = row_dot * factor[:, h * HEAD : h * HEAD + 1]
                expo = e_buf[c, h, qt]
                prob_grad = matmul_t(masked, values)
                score_grad = (expo.astype(F32) * (prob_grad - row_dot)).astype(BF16)
                found.append(matmul(score_grad, keys))
                dk_acc[rows] += matmul(q_t[qt, rows], score_grad)
                dv_acc[rows] += matmul(do_t[rows], expo)
            dq_acc[qt] += jnp.where(first_head, found[0], found[1])
            return carry

        lax.fori_loop(0, 4, block, 0)
        part[c, :, 0] = dk_acc[...].T.astype(BF16).reshape(4, ROWS, PAIR)
        part[c, :, 1] = dv_acc[...].T.astype(BF16).reshape(4, ROWS, PAIR)
        if c:
            send(part.at[c], rs_in.at[c - 1], xs.at[c], xr.at[c], on_patch(z, xc))

    chunk(3)
    weight_b()
    chunk(1)
    weight_c()
    chunk(2)
    weight_d()
    chunk(0)
    for qt in range(4):
        dq_out[qt] = (dq_acc[qt] * (HEAD ** -0.5)).astype(BF16)
    for d in (1, 3, 2):
        to = (z + d) % 4
        send(dq_out.at[to], z_in.at[z, 2], qs.at[d], qr.at[d], on_patch(to, x))
    z_in[z, 2] = dq_out[z]
    weight_e()
    for c in range(1, 4):
        slot = rs_in.at[c - 1]
        remote(slot, slot, xs.at[c], xr.at[c], on_patch(z, right_of(x, c))).wait_recv()
    for d in (1, 3, 2, 0):
        to = (z + d) % 4
        total = part[0, to].astype(F32)
        for c in range(3):
            total = total + rs_in[c, to].astype(F32)
        if d:
            z_out[d - 1] = total.astype(BF16)
            send(z_out.at[d - 1], z_in.at[z, pl.ds(0, 2)], zs.at[d], zr.at[d], on_patch(to, x))
        else:
            z_in[z, pl.ds(0, 2)] = total.astype(BF16)
    weight_out()
    for d in (1, 2, 3):
        at = (z + 4 - d) % 4
        slot = z_in.at[at, 2]
        remote(slot, slot, qs.at[d], qr.at[d], on_patch(at, x)).wait_recv()
        slot = z_in.at[at, pl.ds(0, 2)]
        remote(slot, slot, zs.at[d], zr.at[d], on_patch(at, x)).wait_recv()
    for at in range(4):
        lanes = pl.ds(at * PAIR, PAIR)
        d_keys[:, lanes] = z_in[at, 0].astype(F32)
        d_values[:, lanes] = z_in[at, 1].astype(F32)
        d_queries[:, lanes] = z_in[at, 2].astype(F32)
    for copy in started:
        copy.wait_send()


def right_of(x, c):
    return (x + 4 - OFFSETS[c]) % 4


def call(kernel, outs, ins, scratch, collective_id, flops):
    vmem = pl.BlockSpec(memory_space=pltpu.VMEM)
    hbm = pl.BlockSpec(memory_space=pl.ANY)
    return pl.pallas_call(
        kernel,
        out_shape=[jax.ShapeDtypeStruct(shape, dtype) for shape, dtype, _ in outs],
        in_specs=[vmem if on_chip else hbm for on_chip in ins],
        out_specs=[vmem if on_chip else hbm for _, _, on_chip in outs],
        scratch_shapes=scratch,
        compiler_params=pltpu.CompilerParams(
            collective_id=collective_id, has_side_effects=True, vmem_limit_bytes=VMEM_LIMIT
        ),
        cost_estimate=pl.CostEstimate(flops=flops, bytes_accessed=30_000_000, transcendentals=0),
    )


def dma(*shape):
    return pltpu.SemaphoreType.DMA(shape)


def on_device(patch_queries, patch_keys, patch_values, residual, teacher, output_weight):
    e_shape = (4, 2, 4, ROWS, 1024)
    q2, kv, att_full, att2, fac, expo, t_row, t_ud = call(
        forward_kernel,
        [
            ((4, ROWS, PAIR), BF16, True),
            ((4, 4, 2, ROWS, PAIR), BF16, True),
            ((ROWS, 512), BF16, True),
            ((4, ROWS, PAIR), BF16, True),
            ((4, 4, ROWS, PAIR), F32, True),
            (e_shape, BF16, False),
            ((4, ROWS, 1024), BF16, True),
            ((2, ROWS, 1024), BF16, True),
        ],
        [True] * 4,
        [
            pltpu.VMEM(e_shape, BF16),
            pltpu.VMEM((4, 4, ROWS, PAIR), F32),
            pltpu.VMEM((4, 4, ROWS, PAIR), F32),
            pltpu.VMEM((4, 4, ROWS, PAIR), F32),
            dma(3), dma(3, 4), dma(3, 4), dma(2, 4), dma(2, 4), dma(2, 4), dma(2, 4),
            dma(2), dma(2), dma(2), dma(2), dma(2), dma(2),
            dma(4), dma(4), pltpu.SemaphoreType.DMA, dma(4),
        ],
        0,
        4_000_000_000,
    )(patch_queries[0], patch_keys[0], patch_values[0], teacher[0])
    d_features, datt2, w_term = call(
        gram_kernel,
        [((ROWS, 1024), F32, True), ((4, ROWS, PAIR), BF16, True), ((512, 1024), BF16, True)],
        [True] * 5,
        [
            pltpu.VMEM((4, ROWS, 1024), BF16),
            pltpu.VMEM((2, ROWS, 1024), BF16),
            pltpu.VMEM((2, ROWS, 1024), BF16),
            pltpu.VMEM((2, ROWS, 1024), BF16),
            pltpu.VMEM((ROWS, 512), BF16),
            pltpu.VMEM((ROWS, 1024), F32),
            pltpu.VMEM((ROWS, PAIR), F32),
            dma(2), dma(2), dma(2), dma(2), dma(2), dma(2), dma(2), dma(2),
            dma(4), dma(4), pltpu.SemaphoreType.DMA,
        ],
        1,
        6_000_000_000,
    )(att_full, residual[0], output_weight, t_row, t_ud)
    d_queries, d_keys, d_values, d_weight = call(
        backward_kernel,
        [
            ((ROWS, 512), F32, True),
            ((ROWS, 512), F32, True),
            ((ROWS, 512), F32, True),
            ((512, 1024), F32, True),
        ],
        [True] * 6 + [False],
        [
            pltpu.VMEM(e_shape, BF16),
            pltpu.VMEM((4, PAIR, ROWS), BF16),
            pltpu.VMEM((4, ROWS, PAIR), F32),
            pltpu.VMEM((PAIR, 1024), F32),
            pltpu.VMEM((PAIR, 1024), F32),
            pltpu.VMEM((PAIR, ROWS), BF16),
            pltpu.VMEM((4, 4, 2, ROWS, PAIR), BF16),
            pltpu.VMEM((3, 4, 2, ROWS, PAIR), BF16),
            pltpu.VMEM((3, 2, ROWS, PAIR), BF16),
            pltpu.VMEM((4, 3, ROWS, PAIR), BF16),
            pltpu.VMEM((4, ROWS, PAIR), BF16),
            pltpu.VMEM((7, 64, 1024), BF16),
            pltpu.VMEM((64, 1024), BF16),
            pltpu.VMEM((3, 16, 1024), BF16),
            pltpu.VMEM((16, 1024), BF16),
            pltpu.VMEM((8, 16, 1024), BF16),
            pltpu.VMEM((16, 1024), BF16),
            pltpu.VMEM((4, 16, 1024), BF16),
            pltpu.VMEM((8, 4, 16, 1024), BF16),
            dma(4), dma(4), dma(4), dma(4), dma(4), dma(4), dma(4),
            dma(8), dma(8), dma(4), dma(4), dma(8), dma(8), dma(4), dma(4), dma(8), dma(8),
        ],
        2,
        8_000_000_000,
    )(q2, kv, att2, datt2, fac, w_term, expo)
    return d_queries[None], d_keys[None], d_values[None], d_features[None], d_weight


def solution(mesh):
    placed = P("dp", "patch", None)
    return jax.shard_map(
        on_device,
        mesh=mesh,
        in_specs=(placed,) * 5 + (P(),),
        out_specs=(placed,) * 4 + (P(),),
        check_vma=False,
    )
```

time: 920 us -> 207 us (0.23)
  waiting for transfers between devices: 599 us -> 0 us
  Pallas kernels: 0 us -> 199 us
  matrix products: 144 us -> 0 us
  local copies, waits for them, and re-layouts: 91.1 us -> 7.1 us
  starting transfers between devices: 39.1 us -> 0 us
  other arithmetic: 29 us -> 0 us
  between operations: 14 us -> 0.68 us
    psum x1 -> x0, waiting for transfers between devices: 264 us -> none  [on_device(): d_output_weight = lax.psum(weight_term, ('dp', 'patch'))]
    pallas_call x0 -> x3, Pallas kernels: none -> 199 us  [the longest x1 68.7 us: on_device(): call(forward_kernel, [((4, ROWS, PAIR), BF16, True), ((4, 4, 2, ROWS, PAI...]
    dot_general x73 -> x0, matrix products: 144 us -> none  [the longest x8 30.2 us: forward_block(): jnp.einsum('qhd,khd->hqk', query_heads, block_keys, preferred_element_typ...]
    all_gather x2 -> x0, waiting for transfers between devices: 127 us -> none  [the longest x1 75.5 us: on_device(): lax.all_gather(own_values, 'patch', axis=0, tiled=True)]
    reduce_scatter x1 -> x0, waiting for transfers between devices: 127 us -> none  [on_device(): lax.psum_scatter(joined_terms.astype(jnp.float32).astype(jnp.bfloat16), '...]
    ppermute x9 -> x0, waiting for transfers between devices: 80.6 us -> none  [passed_along(): return lax.ppermute(block, axis, route)]
    ppermute x9 -> x0, starting transfers between devices: 39 us -> none  [passed_along(): return lax.ppermute(block, axis, route)]
    reduce_sum x10 -> x0, other arithmetic: 25.5 us -> none  [the longest x8 24.2 us: forward_block(): running_total = running_total * rescale + jnp.sum(expo, axis=2)]
  transfers between devices with their start and end apart: 13 -> 0, of which waited for: 9 -> 0; matrix products, arithmetic and copies ran while one was open for 5% -> 0% of each run, Pallas kernels for 0% -> 0%
where the time goes in v1:
time: 207 us; the launch traced here: 206 us
  Pallas kernels  199 us (96%)
  local copies, waits for them, and re-layouts  7.1 us (3%)
    pallas_call x1, Pallas kernels, on_device(): call(forward_kernel, [((4, ROWS, PAIR), BF16, True), ((4, 4, 2, ROWS, PAI...  68.7 us
    pallas_call x1, Pallas kernels, on_device(): call(backward_kernel, [((ROWS, 512), F32, True), ((ROWS, 512), F32, True)...  67.6 us
    pallas_call x1, Pallas kernels, on_device(): call(gram_kernel, [((ROWS, 1024), F32, True), ((4, ROWS, PAIR), BF16, Tru...  62.3 us
    unnamed x11, local copies, waits for them, and re-layouts  7.1 us

profile of v1, /device:TPU:2, one launch (start us, length us, event | category | flops | bytes accessed | tf_op | source)
XLA Modules:
  0.0 206.4 jit_solution(1897435129654379813)
XLA Ops:
  0.6 68.7 %shard_map.101 = (bf16[4,256,128]{2,1,0:T(8,128)(2,1)}, bf16[4,4,2,256,128]{4,3,2,1,0:T(8,128)(2,1)}, bf16[256,512]{1,0:T(8,128)(2,1)}, bf16[4,256,128]{2,1,0:T(...) custom-call(bf16[256,512]{1,0:T(8,128)(2,1)} %bitcast.15, ...), custom_call_target="tpu_custom_call" | custom-call | flops 4000000000 | bytes 30000000 | tf_op jit(solution)/shard_map/pallas_call | solution.py:488
  69.4 62.3 %shard_map.102 = (f32[256,1024]{1,0:T(8,128)}, bf16[4,256,128]{2,1,0:T(8,128)(2,1)}, bf16[512,1024]{1,0:T(8,128)(2,1)}) custom-call(bf16[256,512]{1,0:T(8,128)(2,1)} %get-tuple-element.23.att_ref, f32[256,1024]{1,0:T(8,128)} %bitcast.13, bf16[512,1024]{1,0:T(8,128)(2,1)} %w_ref.1, bf16[4,256,1024]{2,1,0:T(8,128)(2,1)} %get-tuple-element.24.t_row, ...), custom_call_target="tpu_custom_call" | custom-call | flops 6000000000 | bytes 30000000 | tf_op jit(solution)/shard_map/pallas_call | solution.py:513
  131.7 67.6 %shard_map.103 = (f32[256,512]{1,0:T(8,128)}, f32[256,512]{1,0:T(8,128)}, f32[256,512]{1,0:T(8,128)}, f32[512,1024]{1,0:T(8,128)}) custom-call(bf16[4,256,128]{2,1,0:T(8,128)(2,1)} %get-tuple-element.20.q2, bf16[4,4,2,256,128]{4,3,2,1,0:T(8,128)(2,1)} %get-tuple-element.21.kv, bf16[4,256,128]{2,1,0:T(8,128)(2,1)} %get-tuple-element.22.att2, ...), custom_call_target="tpu_custom_call" | custom-call | flops 8000000000 | bytes 30000000 | tf_op jit(solution)/shard_map/pallas_call | solution.py:531
  199.3 0.0 copy-start.2
  199.3 0.0 copy-start.1
  199.3 2.0 copy.16
  201.3 0.0 copy-start
  201.3 2.0 copy.17
  203.3 0.0 copy-done.2
  203.3 0.8 copy.18
  204.1 0.0 copy-done.1
  204.1 1.0 copy.19
  205.1 0.0 copy-done
  205.1 1.3 copy.20
Async XLA Ops:
  199.3 4.0 %copy-start.2 = (f32[256,512]{1,0:T(8,128)S(1)}, f32[256,512]{1,0:T(8,128)}, u32[]{:S(2)}) copy-start(f32[256,512]{1,0:T(8,128)} %get-tuple-element.32) | copy-start | bytes 1572868
  199.3 4.8 %copy-start.1 = (f32[256,1024]{1,0:T(8,128)S(1)}, f32[256,1024]{1,0:T(8,128)}, u32[]{:S(2)}) copy-start(f32[256,1024]{1,0:T(8,128)} %get-tuple-element.33) | copy-start | bytes 3145732
  201.3 3.8 %copy-start = (f32[512,1024]{1,0:T(8,128)S(1)}, f32[512,1024]{1,0:T(8,128)}, u32[]{:S(2)}) copy-start(f32[512,1024]{1,0:T(8,128)} %get-tuple-element.44) | copy-start | bytes 6291460

commit v2 on v0

v2 whole, which is shorter than its diff:
```python
from types import SimpleNamespace

import jax
import jax.numpy as jnp
from jax import lax
from jax.experimental import pallas as pl
from jax.experimental.pallas import tpu as pltpu
from jax.sharding import PartitionSpec as P

MESH = pl.DeviceIdType.MESH
F32 = jnp.float32
BF16 = jnp.bfloat16
ROWS = 256
HALF = 128
PAIR = 128
HEAD = 64
D = 1024
KEYS = 1024
PIECES = 2
PIECE = ROWS // PIECES
SCALE = HEAD ** -0.5
OFFSETS = (0, 1, 3, 2)
VMEM_LIMIT = 60 * 1024 * 1024


def dma(*shape):
    return pltpu.SemaphoreType.DMA(shape)


def on_chip(*shape, dtype=BF16):
    return pltpu.VMEM(shape, dtype)


OUTPUTS = {
    "z_in": ((4, 3, ROWS, PAIR), BF16),
    "ge": ((8, 4, 16, D), BF16),
    "d_features": ((ROWS, D), F32),
}
SCRATCH = {
    "t_raw": on_chip(ROWS, D),
    "res": on_chip(ROWS, D, dtype=F32),
    "w": on_chip(512, D),
    "q2": on_chip(4, ROWS, PAIR),
    "kv": on_chip(4, 4, 2, ROWS, PAIR),
    "expo": on_chip(4, 2, 4, ROWS, KEYS),
    "m": on_chip(4, 4, ROWS, PAIR, dtype=F32),
    "l": on_chip(4, 4, ROWS, PAIR, dtype=F32),
    "o": on_chip(4, 4, ROWS, PAIR, dtype=F32),
    "att2": on_chip(4, ROWS, PAIR),
    "att_full": on_chip(ROWS, 512),
    "local": dma(6),
    "qkv_s": dma(3, 4), "qkv_r": dma(3, 4),
    "spread_s": dma(2, 4), "spread_r": dma(2, 4),
    "relay_s": dma(2, 4), "relay_r": dma(2, 4),
    "att_s": dma(4), "att_r": dma(4), "att_own": dma(1),
    "t_row": on_chip(4, ROWS, D),
    "t_sh": on_chip(ROWS, D),
    "t_ext": on_chip(ROWS, D),
    "tile_own": on_chip(ROWS, KEYS, dtype=F32),
    "tile_sh": on_chip(ROWS, KEYS, dtype=F32),
    "s_row": on_chip(4, ROWS, D),
    "s_sh": on_chip(PIECES, PIECE, D),
    "s_ext": on_chip(PIECES, PIECE, D),
    "back_out": on_chip(PIECES, PIECE, D),
    "back_in": on_chip(PIECES, PIECE, D),
    "student": on_chip(ROWS, D, dtype=F32),
    "inverse": on_chip(ROWS, PAIR, dtype=F32),
    "gradient": on_chip(ROWS, D, dtype=F32),
    "grad": on_chip(ROWS, D),
    "datt": on_chip(ROWS, 512),
    "datt2": on_chip(4, ROWS, PAIR),
    "tx_s": dma(2), "tx_r": dma(2), "tr_s": dma(2), "tr_r": dma(2),
    "tz_s": dma(1), "tz_r": dma(1), "te_s": dma(1), "te_r": dma(1),
    "sx_s": dma(2), "sx_r": dma(2), "sr_s": dma(2), "sr_r": dma(2),
    "sz_s": dma(PIECES), "sz_r": dma(PIECES), "se_s": dma(PIECES), "se_r": dma(PIECES),
    "back_s": dma(PIECES), "back_r": dma(PIECES),
    "datt_s": dma(PIECES, 4), "datt_r": dma(PIECES, 4), "datt_own": dma(PIECES),
    "q_t": on_chip(4, PAIR, ROWS),
    "do_t": on_chip(PAIR, ROWS),
    "dq": on_chip(4, ROWS, PAIR, dtype=F32),
    "dk": on_chip(PAIR, KEYS, dtype=F32),
    "dv": on_chip(PAIR, KEYS, dtype=F32),
    "part": on_chip(4, 2, 4, ROWS, PAIR),
    "pass_in": on_chip(2, 4, ROWS, PAIR),
    "sum_in": on_chip(2, 2, 4, ROWS, PAIR),
    "z_out": on_chip(4, 2, ROWS, PAIR),
    "dq_out": on_chip(4, ROWS, PAIR),
    "pass_s": dma(2), "pass_r": dma(2), "sum_s": dma(2), "sum_r": dma(2),
    "zkv_s": dma(4), "zkv_r": dma(4), "zq_s": dma(4), "zq_r": dma(4),
    "w_term": on_chip(512, D),
    "ra": on_chip(7, 64, D), "pa": on_chip(64, D),
    "rb": on_chip(3, 16, D), "pb": on_chip(16, D),
    "rc": on_chip(8, 16, D), "pc": on_chip(16, D),
    "gd": on_chip(4, 16, D),
    "wa_s": dma(8), "wa_r": dma(8), "wb_s": dma(4), "wb_r": dma(4), "wc_s": dma(8), "wc_r": dma(8),
    "wd_s": dma(4), "wd_r": dma(4), "we_s": dma(8), "we_r": dma(8),
}
INPUTS = ("q", "k", "v", "teacher", "residual", "weight")
NAMES = INPUTS + tuple(OUTPUTS) + tuple(SCRATCH)


def on_patch(z, x):
    return {"patch": z * 4 + x}


def remote(src, dst, send_sem, recv_sem, device):
    return pltpu.make_async_remote_copy(
        src_ref=src,
        dst_ref=dst,
        send_sem=send_sem,
        recv_sem=recv_sem,
        device_id=device,
        device_id_type=MESH,
    )


def columns(index):
    return pl.ds(pl.multiple_of(index * PAIR, PAIR), PAIR)


def matmul(a, b):
    return jnp.dot(a, b, preferred_element_type=F32)


def matmul_t(a, b):
    return lax.dot_general(a, b, (((1,), (1,)), ((), ())), preferred_element_type=F32)


def kernel(*refs):
    r = SimpleNamespace(**dict(zip(NAMES, refs, strict=True)))
    index = lax.axis_index("patch")
    z, x = index // 4, index % 4
    dp = lax.axis_index("dp")
    y, z_lo, core = dp // 4, (dp // 2) % 2, dp % 2
    near, ring = y * 2 + core, z * 2 + z_lo
    right, left, across = (x + 1) % 4, (x + 3) % 4, (x + 2) % 4
    high = x // 2
    step = 3 - 2 * high
    shift_to, shift_from = (z + step) % 4, (z + 4 - step) % 4
    swap = x + 1 - 2 * (x % 2)
    inner = (x * (3 - x)) // 2

    def near_device(i):
        return {"dp": (i // 2) * 4 + z_lo * 2 + i % 2}

    def ring_device(i):
        return {"dp": y * 4 + (i % 2) * 2 + core, "patch": (i // 2) * 4 + x}

    started = []

    def send(src, dst, send_sem, recv_sem, device):
        copy = remote(src, dst, send_sem, recv_sem, device)
        copy.start()
        started.append(copy)

    def await_at(slot, send_sem, recv_sem, device):
        remote(slot, slot, send_sem, recv_sem, device).wait_recv()

    local = [
        pltpu.make_async_copy(r.teacher, r.t_raw, r.local.at[0]),
        pltpu.make_async_copy(r.k.at[:, columns(z)], r.kv.at[x, z, 0], r.local.at[1]),
        pltpu.make_async_copy(r.v.at[:, columns(z)], r.kv.at[x, z, 1], r.local.at[2]),
        pltpu.make_async_copy(r.q.at[:, columns(z)], r.q2.at[z], r.local.at[3]),
        pltpu.make_async_copy(r.residual, r.res, r.local.at[4]),
        pltpu.make_async_copy(r.weight, r.w, r.local.at[5]),
    ]
    for copy in local:
        copy.start()
    peers = (
        [ring_device((ring + d) % 8) for d in range(1, 8)]
        + [on_patch(z, (x + d) % 4) for d in range(1, 4)]
        + [near_device((near + d) % 8) for d in range(1, 8)]
    )
    barrier = pltpu.get_barrier_semaphore()
    for peer in peers:
        pl.semaphore_signal(barrier, inc=1, device_id=peer, device_id_type=MESH)
    pl.semaphore_wait(barrier, len(peers))

    for d in (1, 3, 2):
        to = (z + d) % 4
        for i, source in enumerate((r.k, r.v)):
            send(source.at[:, columns(to)], r.kv.at[x, z, i], r.qkv_s.at[i, d], r.qkv_r.at[i, d], on_patch(to, x))
    for d in (1, 3, 2):
        to = (z + d) % 4
        send(r.q.at[:, columns(to)], r.q2.at[z], r.qkv_s.at[2, d], r.qkv_r.at[2, d], on_patch(to, x))

    def spread(d):
        at = (z + 4 - d) % 4
        for side, to in enumerate((right, left)):
            slot = r.kv.at[x, at]
            send(slot, slot, r.spread_s.at[side, d], r.spread_r.at[side, d], on_patch(z, to))

    local[1].wait()
    local[2].wait()
    spread(0)
    local[0].wait()
    teacher = r.t_raw[...].astype(F32)
    r.t_row[x] = (
        teacher * lax.rsqrt(jnp.sum(teacher * teacher, axis=1, keepdims=True) + 1e-06)
    ).astype(BF16)
    for side, to in enumerate((right, left)):
        send(r.t_row.at[x], r.t_row.at[x], r.tx_s.at[side], r.tx_r.at[side], on_patch(z, to))
    for d in (1, 3, 2):
        at = (z + 4 - d) % 4
        for i in range(2):
            await_at(r.kv.at[x, at, i], r.qkv_s.at[i, d], r.qkv_r.at[i, d], on_patch(at, x))
        spread(d)
    send(r.t_row.at[x], r.t_sh, r.tz_s.at[0], r.tz_r.at[0], on_patch(shift_to, x))
    local[3].wait()
    for d in (1, 3, 2):
        at = (z + 4 - d) % 4
        await_at(r.q2.at[at], r.qkv_s.at[2, d], r.qkv_r.at[2, d], on_patch(at, x))

    first_head = lax.broadcasted_iota(jnp.int32, (ROWS, PAIR), 1) < HEAD

    def forward_block(c, qt):
        xc = (x + OFFSETS[c]) % 4
        keys = r.kv[xc, :, 0].reshape(KEYS, PAIR)
        values = r.kv[xc, :, 1].reshape(KEYS, PAIR)
        queries = r.q2[qt].astype(F32) * SCALE
        parts = []
        for h in range(2):
            mask = first_head if h == 0 else jnp.logical_not(first_head)
            masked = jnp.where(mask, queries, 0.0).astype(BF16)
            scores = matmul_t(masked, keys)
            top = jnp.max(scores, axis=1, keepdims=True)
            expo = jnp.exp(scores - top)
            total = jnp.sum(expo, axis=1, keepdims=True)
            rounded = expo.astype(BF16)
            r.expo[c, h, qt] = rounded
            parts.append((top, total, matmul(rounded, values)))
        (m0, l0, o0), (m1, l1, o1) = parts
        r.m[c, qt] = jnp.where(first_head, m0, m1)
        r.l[c, qt] = jnp.where(first_head, l0, l1)
        r.o[c, qt] = jnp.where(first_head, o0, o1)

    def forward_chunk(c):
        def block(qt, carry):
            forward_block(c, qt)
            return carry

        lax.fori_loop(0, 4, block, 0)

    def join(qt):
        tops = [r.m[c, qt] for c in range(4)]
        top = jnp.maximum(jnp.maximum(tops[0], tops[1]), jnp.maximum(tops[2], tops[3]))
        scale = [jnp.exp(tops[c] - top) for c in range(4)]
        total = sum(scale[c] * r.l[c, qt] for c in range(4))
        joined = sum(scale[c] * r.o[c, qt] for c in range(4))
        inverse = 1.0 / total
        r.att2[qt] = (joined * inverse).astype(BF16)
        for c in range(4):
            r.m[c, qt] = scale[c] * inverse

    forward_chunk(0)
    for d in (0, 1, 3, 2):
        at = (z + 4 - d) % 4
        await_at(r.kv.at[right, at], r.spread_s.at[1, d], r.spread_r.at[1, d], on_patch(z, right))
        slot = r.kv.at[right, at, 0]
        send(slot, slot, r.relay_s.at[0, d], r.relay_r.at[0, d], on_patch(z, left))
        await_at(r.kv.at[left, at], r.spread_s.at[0, d], r.spread_r.at[0, d], on_patch(z, left))
        slot = r.kv.at[left, at, 1]
        send(slot, slot, r.relay_s.at[1, d], r.relay_r.at[1, d], on_patch(z, right))
    forward_chunk(1)

    def pass_on(row, x_s, x_r, on_s, on_r):
        await_at(row.at[right], x_s.at[1], x_r.at[1], on_patch(z, right))
        slot = row.at[right, pl.ds(0, HALF)]
        send(slot, slot, on_s.at[0], on_r.at[0], on_patch(z, left))
        await_at(row.at[left], x_s.at[0], x_r.at[0], on_patch(z, left))
        slot = row.at[left, pl.ds(HALF, HALF)]
        send(slot, slot, on_s.at[1], on_r.at[1], on_patch(z, right))

    def await_across(row, on_s, on_r):
        for i in range(2):
            await_at(row.at[across, pl.ds(i * HALF, HALF)], on_s.at[i], on_r.at[i], on_patch(z, right))

    pass_on(r.t_row, r.tx_s, r.tx_r, r.tr_s, r.tr_r)
    forward_chunk(2)
    for d in range(4):
        at = (z + 4 - d) % 4
        for i in range(2):
            await_at(r.kv.at[across, at, i], r.relay_s.at[i, d], r.relay_r.at[i, d], on_patch(z, right))
    for d in (1, 3, 2, 0):
        to = (z + d) % 4
        forward_block(3, to)
        join(to)
        if d:
            send(r.att2.at[to], r.att_full.at[:, columns(z)], r.att_s.at[d], r.att_r.at[d], on_patch(to, x))
    own = pltpu.make_async_copy(r.att2.at[z], r.att_full.at[:, columns(z)], r.att_own.at[0])
    own.start()

    await_at(r.t_sh, r.tz_s.at[0], r.tz_r.at[0], on_patch(shift_from, x))
    send(r.t_sh, r.t_ext, r.te_s.at[0], r.te_r.at[0], on_patch(z, swap))
    own.wait()
    local[4].wait()
    local[5].wait()
    for d in (1, 3, 2):
        at = (z + 4 - d) % 4
        await_at(r.att_full.at[:, columns(at)], r.att_s.at[d], r.att_r.at[d], on_patch(at, x))

    features = r.res[...] + matmul(r.att_full[...], r.w[...])
    inverse = lax.rsqrt(jnp.sum(features * features, axis=1, keepdims=True) + 1e-06)
    student = features * inverse
    r.s_row[x] = student.astype(BF16)
    for p in range(PIECES):
        source = r.s_row.at[x, pl.ds(p * PIECE, PIECE)]
        send(source, r.s_sh.at[p], r.sz_s.at[p], r.sz_r.at[p], on_patch(shift_to, x))
    for side, to in enumerate((right, left)):
        send(r.s_row.at[x], r.s_row.at[x], r.sx_s.at[side], r.sx_r.at[side], on_patch(z, to))
    r.student[...] = student
    r.inverse[...] = jnp.broadcast_to(inverse, (ROWS, PAIR))

    await_across(r.t_row, r.tr_s, r.tr_r)
    r.tile_sh[...] = matmul_t(r.t_sh[...], r.t_row[...].reshape(KEYS, D))
    pass_on(r.s_row, r.sx_s, r.sx_r, r.sr_s, r.sr_r)
    r.tile_own[...] = matmul_t(r.t_row[x], r.t_row[...].reshape(KEYS, D))
    await_across(r.s_row, r.sr_s, r.sr_r)

    first = (1 - high) * (x + 1) * ROWS
    last = KEYS - high * (KEYS - x * ROWS)
    for p in range(PIECES):
        await_at(r.s_sh.at[p], r.sz_s.at[p], r.sz_r.at[p], on_patch(shift_from, x))
        send(r.s_sh.at[p], r.s_ext.at[p], r.se_s.at[p], r.se_r.at[p], on_patch(z, swap))
        row = r.s_row[...].reshape(KEYS, D)
        tile = matmul_t(r.s_sh[p], row) - r.tile_sh[pl.ds(p * PIECE, PIECE)]
        at = lax.broadcasted_iota(jnp.int32, tile.shape, 1)
        tile = jnp.where(jnp.logical_and(at >= first, at < last), tile, 0.0)
        r.back_out[p] = matmul(tile.astype(BF16), row).astype(BF16)
        send(r.back_out.at[p], r.back_in.at[p], r.back_s.at[p], r.back_r.at[p], on_patch(shift_from, x))
    row = r.s_row[...].reshape(KEYS, D)
    own_tile = matmul_t(r.s_row[x], row) - r.tile_own[...]
    r.gradient[...] = matmul(own_tile.astype(BF16), row)
    await_at(r.t_ext, r.te_s.at[0], r.te_r.at[0], on_patch(z, swap))
    for p in range(PIECES):
        await_at(r.s_ext.at[p], r.se_s.at[p], r.se_r.at[p], on_patch(z, swap))
    other = r.s_ext[...].reshape(ROWS, D)
    tile = matmul_t(r.s_row[x], other) - matmul_t(r.t_row[x], r.t_ext[...])
    tile = jnp.where(lax.broadcasted_iota(jnp.int32, tile.shape, 1) < inner * ROWS, tile, 0.0)
    r.gradient[...] += matmul(tile.astype(BF16), other)

    datt_own = []
    for p in range(PIECES):
        rows = pl.ds(p * PIECE, PIECE)
        await_at(r.back_in.at[p], r.back_s.at[p], r.back_r.at[p], on_patch(shift_to, x))
        gram_grad = 32.0 * (r.gradient[rows] + r.back_in[p].astype(F32))
        student = r.student[rows]
        dot = jnp.sum(student * gram_grad, axis=1, keepdims=True)
        grad = r.inverse[rows, :1] * (gram_grad - student * dot)
        r.d_features[rows] = grad
        rounded = grad.astype(BF16)
        r.grad[rows] = rounded
        r.datt[rows] = matmul_t(rounded, r.w[...]).astype(BF16)
        for d in (1, 3, 2):
            to = (z + d) % 4
            source = r.datt.at[rows, columns(to)]
            send(source, r.datt2.at[z, rows], r.datt_s.at[p, d], r.datt_r.at[p, d], on_patch(to, x))
        own = pltpu.make_async_copy(r.datt.at[rows, columns(z)], r.datt2.at[z, rows], r.datt_own.at[p])
        own.start()
        datt_own.append(own)
    transposed = r.att_full[...].astype(F32).T.astype(BF16)
    r.w_term[...] = matmul(transposed, r.grad[...]).astype(BF16)

    def weight_a():
        for d in range(1, 8):
            to = (near + d) % 8
            rows = pl.ds(pl.multiple_of(to * 64, 64), 64)
            send(r.w_term.at[rows], r.ra.at[d - 1], r.wa_s.at[d], r.wa_r.at[d], near_device(to))

    def weight_b():
        total = r.w_term[pl.ds(pl.multiple_of(near * 64, 64), 64)].astype(F32)
        for d in range(1, 8):
            await_at(r.ra.at[d - 1], r.wa_s.at[d], r.wa_r.at[d], near_device((near + d) % 8))
            total = total + r.ra[d - 1].astype(F32)
        r.pa[...] = total.astype(BF16)
        for d in range(1, 4):
            to = (x + d) % 4
            rows = pl.ds(pl.multiple_of(to * 16, 16), 16)
            send(r.pa.at[rows], r.rb.at[d - 1], r.wb_s.at[d], r.wb_r.at[d], on_patch(z, to))

    def weight_c():
        total = r.pa[pl.ds(pl.multiple_of(x * 16, 16), 16)].astype(F32)
        for d in range(1, 4):
            await_at(r.rb.at[d - 1], r.wb_s.at[d], r.wb_r.at[d], on_patch(z, (x + d) % 4))
            total = total + r.rb[d - 1].astype(F32)
        r.pb[...] = total.astype(BF16)
        r.rc[ring] = r.pb[...]
        for d in range(1, 8):
            send(r.pb, r.rc.at[ring], r.wc_s.at[d], r.wc_r.at[d], ring_device((ring + d) % 8))

    def weight_d():
        for d in range(1, 8):
            at = (ring + 8 - d) % 8
            await_at(r.rc.at[at], r.wc_s.at[d], r.wc_r.at[d], ring_device(at))
        total = r.rc[0].astype(F32)
        for i in range(1, 8):
            total = total + r.rc[i].astype(F32)
        r.pc[...] = total.astype(BF16)
        r.gd[x] = r.pc[...]
        for d in range(1, 4):
            send(r.pc, r.gd.at[x], r.wd_s.at[d], r.wd_r.at[d], on_patch(z, (x + d) % 4))

    def weight_e():
        for d in range(1, 4):
            at = (x + 4 - d) % 4
            await_at(r.gd.at[at], r.wd_s.at[d], r.wd_r.at[d], on_patch(z, at))
        r.ge[near] = r.gd[...]
        for d in range(1, 8):
            send(r.gd, r.ge.at[near], r.we_s.at[d], r.we_r.at[d], near_device((near + d) % 8))

    def weight_out():
        for d in range(1, 8):
            at = (near + 8 - d) % 8
            await_at(r.ge.at[at], r.we_s.at[d], r.we_r.at[d], near_device(at))

    weight_a()
    for qt in range(4):
        r.q_t[qt] = (r.q2[qt].astype(F32) * SCALE).T.astype(BF16)
        r.dq[qt] = jnp.zeros((ROWS, PAIR), F32)
    for p in range(PIECES):
        datt_own[p].wait()
        for d in (1, 3, 2):
            at = (z + 4 - d) % 4
            slot = r.datt2.at[at, pl.ds(p * PIECE, PIECE)]
            await_at(slot, r.datt_s.at[p, d], r.datt_r.at[p, d], on_patch(at, x))

    def backward_chunk(c):
        xc = (x + OFFSETS[c]) % 4
        r.dk[...] = jnp.zeros((PAIR, KEYS), F32)
        r.dv[...] = jnp.zeros((PAIR, KEYS), F32)

        def block(qt, carry):
            keys = r.kv[xc, :, 0].reshape(KEYS, PAIR)
            values = r.kv[xc, :, 1].reshape(KEYS, PAIR)
            factor = r.m[c, qt]
            grads = r.datt2[qt].astype(F32)
            scaled = grads * factor
            r.do_t[...] = scaled.T.astype(BF16)
            dots = grads * r.att2[qt].astype(F32)
            found = []
            for h in range(2):
                mask = first_head if h == 0 else jnp.logical_not(first_head)
                rows = pl.ds(h * HEAD, HEAD)
                masked = jnp.where(mask, scaled, 0.0).astype(BF16)
                row_dot = jnp.sum(jnp.where(mask, dots, 0.0), axis=1, keepdims=True)
                row_dot = row_dot * factor[:, h * HEAD : h * HEAD + 1]
                expo = r.expo[c, h, qt]
                prob_grad = matmul_t(masked, values)
                score_grad = (expo.astype(F32) * (prob_grad - row_dot)).astype(BF16)
                found.append(matmul(score_grad, keys))
                r.dk[rows] += matmul(r.q_t[qt, rows], score_grad)
                r.dv[rows] += matmul(r.do_t[rows], expo)
            r.dq[qt] += jnp.where(first_head, found[0], found[1])
            return carry

        lax.fori_loop(0, 4, block, 0)
        return r.dk[...].T.reshape(4, ROWS, PAIR), r.dv[...].T.reshape(4, ROWS, PAIR)

    dk, dv = backward_chunk(3)
    r.part[3, 0], r.part[3, 1] = dk.astype(BF16), dv.astype(BF16)
    send(r.part.at[3, 0], r.pass_in.at[0], r.pass_s.at[0], r.pass_r.at[0], on_patch(z, right))
    send(r.part.at[3, 1], r.pass_in.at[1], r.pass_s.at[1], r.pass_r.at[1], on_patch(z, left))
    weight_b()
    dk, dv = backward_chunk(1)
    await_at(r.pass_in.at[0], r.pass_s.at[0], r.pass_r.at[0], on_patch(z, left))
    r.part[1, 0], r.part[1, 1] = (dk + r.pass_in[0].astype(F32)).astype(BF16), dv.astype(BF16)
    send(r.part.at[1], r.sum_in.at[0], r.sum_s.at[0], r.sum_r.at[0], on_patch(z, right))
    weight_c()
    dk, dv = backward_chunk(2)
    await_at(r.pass_in.at[1], r.pass_s.at[1], r.pass_r.at[1], on_patch(z, right))
    r.part[2, 0], r.part[2, 1] = dk.astype(BF16), (dv + r.pass_in[1].astype(F32)).astype(BF16)
    send(r.part.at[2], r.sum_in.at[1], r.sum_s.at[1], r.sum_r.at[1], on_patch(z, left))
    weight_d()
    dk, dv = backward_chunk(0)
    r.part[0, 0], r.part[0, 1] = dk.astype(BF16), dv.astype(BF16)
    for d in (1, 3, 2, 0):
        to = (z + d) % 4
        r.dq_out[to] = (r.dq[to] * SCALE).astype(BF16)
        if d:
            send(r.dq_out.at[to], r.z_in.at[z, 2], r.zq_s.at[d], r.zq_r.at[d], on_patch(to, x))
        else:
            r.z_in[z, 2] = r.dq_out[z]
    weight_e()
    await_at(r.sum_in.at[0], r.sum_s.at[0], r.sum_r.at[0], on_patch(z, left))
    await_at(r.sum_in.at[1], r.sum_s.at[1], r.sum_r.at[1], on_patch(z, right))
    for d in (1, 3, 2, 0):
        to = (z + d) % 4
        for i in range(2):
            total = r.part[0, i, to].astype(F32)
            total = total + r.sum_in[0, i, to].astype(F32) + r.sum_in[1, i, to].astype(F32)
            if d:
                r.z_out[d, i] = total.astype(BF16)
            else:
                r.z_in[z, i] = total.astype(BF16)
        if d:
            send(r.z_out.at[d], r.z_in.at[z, pl.ds(0, 2)], r.zkv_s.at[d], r.zkv_r.at[d], on_patch(to, x))
    weight_out()
    for d in (1, 3, 2):
        at = (z + 4 - d) % 4
        await_at(r.z_in.at[at, 2], r.zq_s.at[d], r.zq_r.at[d], on_patch(at, x))
        await_at(r.z_in.at[at, pl.ds(0, 2)], r.zkv_s.at[d], r.zkv_r.at[d], on_patch(at, x))
    for copy in started:
        copy.wait_send()


def finish(z_in, weight, features, d_queries, d_keys, d_values, d_weight, d_features):
    d_keys[...] = z_in[0, 0].astype(F32)
    d_values[...] = z_in[0, 1].astype(F32)
    d_queries[...] = z_in[0, 2].astype(F32)
    d_weight[...] = weight[...].astype(F32)
    d_features[...] = features[...]


def on_device(patch_queries, patch_keys, patch_values, residual, teacher, output_weight):
    vmem = pl.BlockSpec(memory_space=pltpu.VMEM)
    hbm = pl.BlockSpec(memory_space=pl.ANY)
    z_in, weight, features = pl.pallas_call(
        kernel,
        out_shape=[jax.ShapeDtypeStruct(shape, dtype) for shape, dtype in OUTPUTS.values()],
        in_specs=[hbm] * 6,
        out_specs=[vmem] * 3,
        scratch_shapes=list(SCRATCH.values()),
        compiler_params=pltpu.CompilerParams(
            collective_id=0, has_side_effects=True, vmem_limit_bytes=VMEM_LIMIT
        ),
        cost_estimate=pl.CostEstimate(
            flops=18_000_000_000, bytes_accessed=10_000_000, transcendentals=9_000_000
        ),
    )(patch_queries[0], patch_keys[0], patch_values[0], teacher[0], residual[0], output_weight)
    head_columns = pl.BlockSpec((ROWS, PAIR), lambda i: (0, i))
    d_queries, d_keys, d_values, d_weight, d_features = pl.pallas_call(
        finish,
        grid=(4,),
        out_shape=[jax.ShapeDtypeStruct((ROWS, 512), F32)] * 3
        + [jax.ShapeDtypeStruct((512, D), F32), jax.ShapeDtypeStruct((ROWS, D), F32)],
        in_specs=[
            pl.BlockSpec((1, 3, ROWS, PAIR), lambda i: (i, 0, 0, 0)),
            pl.BlockSpec((PAIR, D), lambda i: (i, 0)),
            pl.BlockSpec((64, D), lambda i: (i, 0)),
        ],
        out_specs=[head_columns] * 3
        + [pl.BlockSpec((PAIR, D), lambda i: (i, 0)), pl.BlockSpec((64, D), lambda i: (i, 0))],
    )(z_in, weight.reshape(512, D), features)
    return d_queries[None], d_keys[None], d_values[None], d_features[None], d_weight


def solution(mesh):
    placed = P("dp", "patch", None)
    return jax.shard_map(
        on_device,
        mesh=mesh,
        in_specs=(placed,) * 5 + (P(),),
        out_specs=(placed,) * 4 + (P(),),
        check_vma=False,
    )
```

time: 920 us -> 174 us (0.19)
  waiting for transfers between devices: 599 us -> 0 us
  Pallas kernels: 0 us -> 170 us
  matrix products: 144 us -> 0 us
  local copies, waits for them, and re-layouts: 91.1 us -> 0 us
  starting transfers between devices: 39.1 us -> 0 us
  other arithmetic: 29 us -> 0 us
  between operations: 14 us -> 0.7 us
    psum x1 -> x0, waiting for transfers between devices: 264 us -> none  [on_device(): d_output_weight = lax.psum(weight_term, ('dp', 'patch'))]
    pallas_call x0 -> x2, Pallas kernels: none -> 170 us  [the longest x1 166 us: on_device(): pl.pallas_call(kernel, out_shape=[jax.ShapeDtypeStruct(shape, dtype) for...]
    dot_general x73 -> x0, matrix products: 144 us -> none  [the longest x8 30.2 us: forward_block(): jnp.einsum('qhd,khd->hqk', query_heads, block_keys, preferred_element_typ...]
    all_gather x2 -> x0, waiting for transfers between devices: 127 us -> none  [the longest x1 75.5 us: on_device(): lax.all_gather(own_values, 'patch', axis=0, tiled=True)]
    reduce_scatter x1 -> x0, waiting for transfers between devices: 127 us -> none  [on_device(): lax.psum_scatter(joined_terms.astype(jnp.float32).astype(jnp.bfloat16), '...]
    ppermute x9 -> x0, waiting for transfers between devices: 80.6 us -> none  [passed_along(): return lax.ppermute(block, axis, route)]
    ppermute x9 -> x0, starting transfers between devices: 39 us -> none  [passed_along(): return lax.ppermute(block, axis, route)]
    unnamed x27 -> x0, local copies, waits for them, and re-layouts: 26.9 us -> none
  transfers between devices with their start and end apart: 13 -> 0, of which waited for: 9 -> 0; matrix products, arithmetic and copies ran while one was open for 5% -> 0% of each run, Pallas kernels for 0% -> 0%
where the time goes in v2:
time: 174 us; the launch traced here: 171 us
  Pallas kernels  170 us (98%)
    pallas_call x1, Pallas kernels, on_device(): pl.pallas_call(kernel, out_shape=[jax.ShapeDtypeStruct(shape, dtype) for...  166 us
    pallas_call x1, Pallas kernels, on_device(): pl.pallas_call(finish, grid=(4,), out_shape=[jax.ShapeDtypeStruct((ROWS,...  4.47 us

profile of v2, /device:TPU:2, one launch (start us, length us, event | category | flops | bytes accessed | tf_op | source)
XLA Modules:
  0.0 171.1 jit_solution(341009180988043370)
XLA Ops:
  0.6 165.9 %shard_map.101 = (bf16[4,3,256,128]{3,2,1,0:T(8,128)(2,1)}, bf16[8,4,16,1024]{3,2,1,0:T(8,128)(2,1)}, f32[256,1024]{1,0:T(8,128)}) custom-call(bf16[256,512]{1,0:T(8,128)(2,1)} %bitcast.17, bf16[256,512]{1,0:T(8,128)(2,1)} %bitcast.18, bf16[256,512]{1,0:T(8,128)(2,1)} %bitcast.19, bf16[256,1024]{1,0:T(8,128)(2,1)} %bitcast.13, f32[256,1024]{1,0:T(8,128)} %bitcast.11, ...), custom_call_target="tpu_custom_call" | custom-call | flops 17999998976 | bytes 10000000 | tf_op jit(solution)/shard_map/pallas_call | solution.py:517
  166.5 4.5 %shard_map.102 = (f32[256,512]{1,0:T(8,128)}, f32[256,512]{1,0:T(8,128)}, f32[256,512]{1,0:T(8,128)}, f32[512,1024]{1,0:T(8,128)}, f32[256,1024]{1,0:T(8,128)}) custom-call(bf16[4,3,256,128]{3,2,1,0:T(8,128)(2,1)} %get-tuple-element.13.z_in, bf16[512,1024]{1,0:T(8,128)(2,1)} %bitcast.10, f32[256,1024]{1,0:T(8,128)} %get-tuple-element.15.features), custom_call_target="tpu_custom_call" | custom-call | tf_op jit(solution)/shard_map/pallas_call | solution.py:531

commit v3 on v2

v3 whole, which is shorter than its diff:
```python
from types import SimpleNamespace

import jax
import jax.numpy as jnp
from jax import lax
from jax.experimental import pallas as pl
from jax.experimental.pallas import tpu as pltpu
from jax.sharding import PartitionSpec as P

MESH = pl.DeviceIdType.MESH
F32 = jnp.float32
BF16 = jnp.bfloat16
ROWS = 256
HALF = 128
PAIR = 128
HEAD = 64
D = 1024
KEYS = 1024
QUERIES = 512
SCALE = HEAD ** -0.5
OFFSETS = (0, 1, 3, 2)
VMEM_LIMIT = 60 * 1024 * 1024


def dma(*shape):
    return pltpu.SemaphoreType.DMA(shape)


def on_chip(*shape, dtype=BF16):
    return pltpu.VMEM(shape, dtype)


OUTPUTS = {
    "z_in": ((4, 3, 2, HALF, PAIR), BF16),
    "ge": ((8, 4, 16, D), BF16),
    "d_features": ((ROWS, D), F32),
}
SCRATCH = {
    "t_raw": on_chip(ROWS, D),
    "res": on_chip(ROWS, D, dtype=F32),
    "w": on_chip(512, D),
    "q2": on_chip(2, 4, HALF, PAIR),
    "kv": on_chip(4, 2, 4, 2, HALF, PAIR),
    "expo": on_chip(4, 2, 2, 4, HALF, KEYS),
    "m": on_chip(4, 2, 4, HALF, PAIR, dtype=F32),
    "l": on_chip(4, 2, 4, HALF, PAIR, dtype=F32),
    "o": on_chip(4, 2, 4, HALF, PAIR, dtype=F32),
    "att2": on_chip(2, 4, HALF, PAIR),
    "att_full": on_chip(ROWS, 512),
    "local": dma(6),
    "qkv_s": dma(3, 4), "qkv_r": dma(3, 4),
    "spread_s": dma(2, 4), "spread_r": dma(2, 4),
    "relay_s": dma(2, 4), "relay_r": dma(2, 4),
    "att_s": dma(2, 4), "att_r": dma(2, 4), "att_own": dma(2),
    "t_row": on_chip(4, ROWS, D),
    "t_sh": on_chip(ROWS, D),
    "t_ext": on_chip(ROWS, D),
    "tile_own": on_chip(ROWS, KEYS, dtype=F32),
    "tile_sh": on_chip(ROWS, KEYS, dtype=F32),
    "s_row": on_chip(4, ROWS, D),
    "s_sh": on_chip(2, HALF, D),
    "s_ext": on_chip(2, HALF, D),
    "back_out": on_chip(2, HALF, D),
    "back_in": on_chip(2, HALF, D),
    "student": on_chip(ROWS, D, dtype=F32),
    "inverse": on_chip(ROWS, PAIR, dtype=F32),
    "gradient": on_chip(ROWS, D, dtype=F32),
    "grad": on_chip(ROWS, D),
    "datt": on_chip(ROWS, 512),
    "datt2": on_chip(2, 4, HALF, PAIR),
    "tx_s": dma(2), "tx_r": dma(2), "tr_s": dma(2), "tr_r": dma(2),
    "tz_s": dma(1), "tz_r": dma(1), "te_s": dma(1), "te_r": dma(1),
    "sx_s": dma(2, 2), "sx_r": dma(2, 2), "sr_s": dma(2), "sr_r": dma(2),
    "sz_s": dma(2), "sz_r": dma(2), "se_s": dma(2), "se_r": dma(2),
    "back_s": dma(2), "back_r": dma(2),
    "datt_s": dma(2, 4), "datt_r": dma(2, 4), "datt_own": dma(2),
    "q_t": on_chip(2, PAIR, QUERIES),
    "do_m": on_chip(4, 2, 2, QUERIES, PAIR),
    "do_t": on_chip(4, 2, PAIR, QUERIES),
    "dots": on_chip(4, 2, QUERIES, PAIR, dtype=F32),
    "dq": on_chip(2, QUERIES, PAIR, dtype=F32),
    "dk": on_chip(PAIR, QUERIES, dtype=F32),
    "dv": on_chip(PAIR, QUERIES, dtype=F32),
    "part": on_chip(2, 4, 2, 4, HALF, PAIR),
    "pass_in": on_chip(2, 2, 4, HALF, PAIR),
    "sum_in": on_chip(2, 2, 2, 4, HALF, PAIR),
    "z_out": on_chip(2, 4, 2, HALF, PAIR),
    "dq_out": on_chip(4, 2, HALF, PAIR),
    "pass_s": dma(2, 2), "pass_r": dma(2, 2), "sum_s": dma(2, 2), "sum_r": dma(2, 2),
    "zkv_s": dma(2, 4), "zkv_r": dma(2, 4), "zq_s": dma(4), "zq_r": dma(4),
    "w_term": on_chip(512, D),
    "ra": on_chip(7, 64, D), "pa": on_chip(64, D),
    "rb": on_chip(3, 16, D), "pb": on_chip(16, D),
    "rc": on_chip(8, 16, D), "pc": on_chip(16, D),
    "gd": on_chip(4, 16, D),
    "wa_s": dma(8), "wa_r": dma(8), "wb_s": dma(4), "wb_r": dma(4), "wc_s": dma(8), "wc_r": dma(8),
    "wd_s": dma(4), "wd_r": dma(4), "we_s": dma(8), "we_r": dma(8),
}
INPUTS = ("q", "k", "v", "teacher", "residual", "weight")
NAMES = INPUTS + tuple(OUTPUTS) + tuple(SCRATCH)


def on_patch(z, x):
    return {"patch": z * 4 + x}


def remote(src, dst, send_sem, recv_sem, device):
    return pltpu.make_async_remote_copy(
        src_ref=src,
        dst_ref=dst,
        send_sem=send_sem,
        recv_sem=recv_sem,
        device_id=device,
        device_id_type=MESH,
    )


def columns(index):
    return pl.ds(pl.multiple_of(index * PAIR, PAIR), PAIR)


def matmul(a, b):
    return jnp.dot(a, b, preferred_element_type=F32)


def matmul_t(a, b):
    return lax.dot_general(a, b, (((1,), (1,)), ((), ())), preferred_element_type=F32)


def kernel(*refs):
    r = SimpleNamespace(**dict(zip(NAMES, refs, strict=True)))
    index = lax.axis_index("patch")
    z, x = index // 4, index % 4
    dp = lax.axis_index("dp")
    y, z_lo, core = dp // 4, (dp // 2) % 2, dp % 2
    near, ring = y * 2 + core, z * 2 + z_lo
    right, left, across = (x + 1) % 4, (x + 3) % 4, (x + 2) % 4
    high = x // 2
    step = 3 - 2 * high
    shift_to, shift_from = (z + step) % 4, (z + 4 - step) % 4
    swap = x + 1 - 2 * (x % 2)
    inner = (x * (3 - x)) // 2

    def near_device(i):
        return {"dp": (i // 2) * 4 + z_lo * 2 + i % 2}

    def ring_device(i):
        return {"dp": y * 4 + (i % 2) * 2 + core, "patch": (i // 2) * 4 + x}

    started = []

    def send(src, dst, send_sem, recv_sem, device):
        copy = remote(src, dst, send_sem, recv_sem, device)
        copy.start()
        started.append(copy)

    def await_at(slot, send_sem, recv_sem, device):
        remote(slot, slot, send_sem, recv_sem, device).wait_recv()

    local = [
        pltpu.make_async_copy(r.teacher, r.t_raw, r.local.at[0]),
        pltpu.make_async_copy(r.k.at[:, :, columns(z)], r.kv.at[x, :, z, 0], r.local.at[1]),
        pltpu.make_async_copy(r.v.at[:, :, columns(z)], r.kv.at[x, :, z, 1], r.local.at[2]),
        pltpu.make_async_copy(r.q.at[:, :, columns(z)], r.q2.at[:, z], r.local.at[3]),
        pltpu.make_async_copy(r.residual, r.res, r.local.at[4]),
        pltpu.make_async_copy(r.weight, r.w, r.local.at[5]),
    ]
    for copy in local:
        copy.start()
    peers = (
        [ring_device((ring + d) % 8) for d in range(1, 8)]
        + [on_patch(z, (x + d) % 4) for d in range(1, 4)]
        + [near_device((near + d) % 8) for d in range(1, 8)]
    )
    barrier = pltpu.get_barrier_semaphore()
    for peer in peers:
        pl.semaphore_signal(barrier, inc=1, device_id=peer, device_id_type=MESH)
    pl.semaphore_wait(barrier, len(peers))

    for d in (1, 3, 2):
        to = (z + d) % 4
        for i, source in enumerate((r.k, r.v)):
            send(source.at[:, :, columns(to)], r.kv.at[x, :, z, i], r.qkv_s.at[i, d], r.qkv_r.at[i, d], on_patch(to, x))
    for d in (1, 3, 2):
        to = (z + d) % 4
        send(r.q.at[:, :, columns(to)], r.q2.at[:, z], r.qkv_s.at[2, d], r.qkv_r.at[2, d], on_patch(to, x))

    def spread(d):
        at = (z + 4 - d) % 4
        for side, to in enumerate((right, left)):
            slot = r.kv.at[x, :, at]
            send(slot, slot, r.spread_s.at[side, d], r.spread_r.at[side, d], on_patch(z, to))

    local[1].wait()
    local[2].wait()
    spread(0)
    local[0].wait()
    teacher = r.t_raw[...].astype(F32)
    r.t_row[x] = (
        teacher * lax.rsqrt(jnp.sum(teacher * teacher, axis=1, keepdims=True) + 1e-06)
    ).astype(BF16)
    for side, to in enumerate((right, left)):
        send(r.t_row.at[x], r.t_row.at[x], r.tx_s.at[side], r.tx_r.at[side], on_patch(z, to))
    for d in (1, 3, 2):
        at = (z + 4 - d) % 4
        for i in range(2):
            await_at(r.kv.at[x, :, at, i], r.qkv_s.at[i, d], r.qkv_r.at[i, d], on_patch(at, x))
        spread(d)
    send(r.t_row.at[x], r.t_sh, r.tz_s.at[0], r.tz_r.at[0], on_patch(shift_to, x))
    local[3].wait()
    for d in (1, 3, 2):
        at = (z + 4 - d) % 4
        await_at(r.q2.at[:, at], r.qkv_s.at[2, d], r.qkv_r.at[2, d], on_patch(at, x))

    def first_head(rows):
        return lax.broadcasted_iota(jnp.int32, (rows, PAIR), 1) < HEAD

    def of_head(h, block):
        mask = first_head(block.shape[0])
        return jnp.where(mask if h == 0 else jnp.logical_not(mask), block, 0.0)

    def forward_block(c, half, blocks):
        xc = (x + OFFSETS[c]) % 4
        keys = r.kv[xc, :, :, 0].reshape(KEYS, PAIR)
        values = r.kv[xc, :, :, 1].reshape(KEYS, PAIR)
        queries = jnp.concatenate([r.q2[half, qt] for qt in blocks], axis=0).astype(F32) * SCALE
        parts = []
        for h in range(2):
            scores = matmul_t(of_head(h, queries).astype(BF16), keys)
            top = jnp.max(scores, axis=1, keepdims=True)
            expo = jnp.exp(scores - top)
            total = jnp.sum(expo, axis=1, keepdims=True)
            rounded = expo.astype(BF16)
            for i, qt in enumerate(blocks):
                r.expo[c, h, half, qt] = rounded[i * HALF : (i + 1) * HALF]
            parts.append((top, total, matmul(rounded, values)))
        for ref, first, second in zip((r.m, r.l, r.o), *parts):
            both = jnp.where(first_head(ROWS), first, second)
            for i, qt in enumerate(blocks):
                ref[c, half, qt] = both[i * HALF : (i + 1) * HALF]

    def forward_part(c, half):
        def block(pair, carry):
            forward_block(c, half, (2 * pair, 2 * pair + 1))
            return carry

        lax.fori_loop(0, 2, block, 0)

    def join(half, qt):
        tops = [r.m[c, half, qt] for c in range(4)]
        top = jnp.maximum(jnp.maximum(tops[0], tops[1]), jnp.maximum(tops[2], tops[3]))
        scale = [jnp.exp(tops[c] - top) for c in range(4)]
        total = sum(scale[c] * r.l[c, half, qt] for c in range(4))
        joined = sum(scale[c] * r.o[c, half, qt] for c in range(4))
        inverse = 1.0 / total
        r.att2[half, qt] = (joined * inverse).astype(BF16)
        for c in range(4):
            r.m[c, half, qt] = scale[c] * inverse

    att_own = []

    def forward_last(half):
        rows = pl.ds(half * HALF, HALF)
        for pair in ((1, 2), (3, 0)):
            forward_block(3, half, tuple((z + d) % 4 for d in pair))
            for d in pair:
                to = (z + d) % 4
                join(half, to)
                source, target = r.att2.at[half, to], r.att_full.at[rows, columns(z)]
                if d:
                    send(source, target, r.att_s.at[half, d], r.att_r.at[half, d], on_patch(to, x))
                else:
                    own = pltpu.make_async_copy(source, target, r.att_own.at[half])
                    own.start()
                    att_own.append(own)

    def features(half):
        rows = pl.ds(half * HALF, HALF)
        att_own[half].wait()
        for d in (1, 3, 2):
            at = (z + 4 - d) % 4
            slot = r.att_full.at[rows, columns(at)]
            await_at(slot, r.att_s.at[half, d], r.att_r.at[half, d], on_patch(at, x))
        values = r.res[rows] + matmul(r.att_full[rows], r.w[...])
        inverse = lax.rsqrt(jnp.sum(values * values, axis=1, keepdims=True) + 1e-06)
        student = values * inverse
        r.s_row[x, rows] = student.astype(BF16)
        source = r.s_row.at[x, rows]
        send(source, r.s_sh.at[half], r.sz_s.at[half], r.sz_r.at[half], on_patch(shift_to, x))
        for side, to in enumerate((right, left)):
            send(source, source, r.sx_s.at[side, half], r.sx_r.at[side, half], on_patch(z, to))
        r.student[rows] = student
        r.inverse[rows] = jnp.broadcast_to(inverse, (HALF, PAIR))

    def pass_students(half):
        rows = pl.ds(half * HALF, HALF)
        for side, origin, to in ((1, right, left), (0, left, right)):
            slot = r.s_row.at[origin, rows]
            await_at(slot, r.sx_s.at[side, half], r.sx_r.at[side, half], on_patch(z, origin))
            if side != half:
                send(slot, slot, r.sr_s.at[half], r.sr_r.at[half], on_patch(z, to))

    def swap_students(half):
        slot = r.s_sh.at[half]
        await_at(slot, r.sz_s.at[half], r.sz_r.at[half], on_patch(shift_from, x))
        send(slot, r.s_ext.at[half], r.se_s.at[half], r.se_r.at[half], on_patch(z, swap))

    for half in range(2):
        forward_part(0, half)
    for d in (0, 1, 3, 2):
        at = (z + 4 - d) % 4
        for side, origin, to in ((1, right, left), (0, left, right)):
            await_at(r.kv.at[origin, :, at], r.spread_s.at[side, d], r.spread_r.at[side, d], on_patch(z, origin))
            slot = r.kv.at[origin, :, at, 1 - side]
            send(slot, slot, r.relay_s.at[1 - side, d], r.relay_r.at[1 - side, d], on_patch(z, to))
    forward_part(1, 0)
    for side, origin, to in ((1, right, left), (0, left, right)):
        await_at(r.t_row.at[origin], r.tx_s.at[side], r.tx_r.at[side], on_patch(z, origin))
        slot = r.t_row.at[origin, pl.ds((1 - side) * HALF, HALF)]
        send(slot, slot, r.tr_s.at[1 - side], r.tr_r.at[1 - side], on_patch(z, to))
    forward_part(2, 0)
    for d in range(4):
        at = (z + 4 - d) % 4
        for i in range(2):
            await_at(r.kv.at[across, :, at, i], r.relay_s.at[i, d], r.relay_r.at[i, d], on_patch(z, right))
    forward_last(0)
    forward_part(1, 1)
    local[4].wait()
    local[5].wait()
    features(0)
    forward_part(2, 1)
    pass_students(0)
    forward_last(1)
    await_at(r.t_sh, r.tz_s.at[0], r.tz_r.at[0], on_patch(shift_from, x))
    send(r.t_sh, r.t_ext, r.te_s.at[0], r.te_r.at[0], on_patch(z, swap))
    swap_students(0)
    features(1)

    for i in range(2):
        await_at(r.t_row.at[across, pl.ds(i * HALF, HALF)], r.tr_s.at[i], r.tr_r.at[i], on_patch(z, right))
    r.tile_sh[...] = matmul_t(r.t_sh[...], r.t_row[...].reshape(KEYS, D))
    pass_students(1)
    r.tile_own[...] = matmul_t(r.t_row[x], r.t_row[...].reshape(KEYS, D))
    for i in range(2):
        await_at(r.s_row.at[across, pl.ds(i * HALF, HALF)], r.sr_s.at[i], r.sr_r.at[i], on_patch(z, right))

    first = (1 - high) * (x + 1) * ROWS
    last = KEYS - high * (KEYS - x * ROWS)
    for p in range(2):
        if p:
            swap_students(p)
        row = r.s_row[...].reshape(KEYS, D)
        tile = matmul_t(r.s_sh[p], row) - r.tile_sh[pl.ds(p * HALF, HALF)]
        at = lax.broadcasted_iota(jnp.int32, tile.shape, 1)
        tile = jnp.where(jnp.logical_and(at >= first, at < last), tile, 0.0)
        r.back_out[p] = matmul(tile.astype(BF16), row).astype(BF16)
        send(r.back_out.at[p], r.back_in.at[p], r.back_s.at[p], r.back_r.at[p], on_patch(shift_from, x))
    row = r.s_row[...].reshape(KEYS, D)
    own_tile = matmul_t(r.s_row[x], row) - r.tile_own[...]
    r.gradient[...] = matmul(own_tile.astype(BF16), row)
    await_at(r.t_ext, r.te_s.at[0], r.te_r.at[0], on_patch(z, swap))
    for p in range(2):
        await_at(r.s_ext.at[p], r.se_s.at[p], r.se_r.at[p], on_patch(z, swap))
    other = r.s_ext[...].reshape(ROWS, D)
    tile = matmul_t(r.s_row[x], other) - matmul_t(r.t_row[x], r.t_ext[...])
    tile = jnp.where(lax.broadcasted_iota(jnp.int32, tile.shape, 1) < inner * ROWS, tile, 0.0)
    r.gradient[...] += matmul(tile.astype(BF16), other)

    datt_own = []
    for p in range(2):
        rows = pl.ds(p * HALF, HALF)
        await_at(r.back_in.at[p], r.back_s.at[p], r.back_r.at[p], on_patch(shift_to, x))
        gram_grad = 32.0 * (r.gradient[rows] + r.back_in[p].astype(F32))
        student = r.student[rows]
        dot = jnp.sum(student * gram_grad, axis=1, keepdims=True)
        grad = r.inverse[rows, :1] * (gram_grad - student * dot)
        r.d_features[rows] = grad
        rounded = grad.astype(BF16)
        r.grad[rows] = rounded
        r.datt[rows] = matmul_t(rounded, r.w[...]).astype(BF16)
        for d in (1, 3, 2):
            to = (z + d) % 4
            source = r.datt.at[rows, columns(to)]
            send(source, r.datt2.at[p, z], r.datt_s.at[p, d], r.datt_r.at[p, d], on_patch(to, x))
        own = pltpu.make_async_copy(r.datt.at[rows, columns(z)], r.datt2.at[p, z], r.datt_own.at[p])
        own.start()
        datt_own.append(own)
    transposed = r.att_full[...].astype(F32).T.astype(BF16)
    r.w_term[...] = matmul(transposed, r.grad[...]).astype(BF16)

    def weight_a():
        for d in range(1, 8):
            to = (near + d) % 8
            rows = pl.ds(pl.multiple_of(to * 64, 64), 64)
            send(r.w_term.at[rows], r.ra.at[d - 1], r.wa_s.at[d], r.wa_r.at[d], near_device(to))

    def weight_b():
        total = r.w_term[pl.ds(pl.multiple_of(near * 64, 64), 64)].astype(F32)
        for d in range(1, 8):
            await_at(r.ra.at[d - 1], r.wa_s.at[d], r.wa_r.at[d], near_device((near + d) % 8))
            total = total + r.ra[d - 1].astype(F32)
        r.pa[...] = total.astype(BF16)
        for d in range(1, 4):
            to = (x + d) % 4
            rows = pl.ds(pl.multiple_of(to * 16, 16), 16)
            send(r.pa.at[rows], r.rb.at[d - 1], r.wb_s.at[d], r.wb_r.at[d], on_patch(z, to))

    def weight_c():
        total = r.pa[pl.ds(pl.multiple_of(x * 16, 16), 16)].astype(F32)
        for d in range(1, 4):
            await_at(r.rb.at[d - 1], r.wb_s.at[d], r.wb_r.at[d], on_patch(z, (x + d) % 4))
            total = total + r.rb[d - 1].astype(F32)
        r.pb[...] = total.astype(BF16)
        r.rc[ring] = r.pb[...]
        for d in range(1, 8):
            send(r.pb, r.rc.at[ring], r.wc_s.at[d], r.wc_r.at[d], ring_device((ring + d) % 8))

    def weight_d():
        for d in range(1, 8):
            at = (ring + 8 - d) % 8
            await_at(r.rc.at[at], r.wc_s.at[d], r.wc_r.at[d], ring_device(at))
        total = r.rc[0].astype(F32)
        for i in range(1, 8):
            total = total + r.rc[i].astype(F32)
        r.pc[...] = total.astype(BF16)
        r.gd[x] = r.pc[...]
        for d in range(1, 4):
            send(r.pc, r.gd.at[x], r.wd_s.at[d], r.wd_r.at[d], on_patch(z, (x + d) % 4))

    def weight_e():
        for d in range(1, 4):
            at = (x + 4 - d) % 4
            await_at(r.gd.at[at], r.wd_s.at[d], r.wd_r.at[d], on_patch(z, at))
        r.ge[near] = r.gd[...]
        for d in range(1, 8):
            send(r.gd, r.ge.at[near], r.we_s.at[d], r.we_r.at[d], near_device((near + d) % 8))

    def weight_out():
        for d in range(1, 8):
            at = (near + 8 - d) % 8
            await_at(r.ge.at[at], r.we_s.at[d], r.we_r.at[d], near_device(at))

    weight_a()
    for half in range(2):
        r.q_t[half] = (r.q2[half].reshape(QUERIES, PAIR).astype(F32) * SCALE).T.astype(BF16)
        r.dq[half] = jnp.zeros((QUERIES, PAIR), F32)

    def await_grads(p):
        datt_own[p].wait()
        for d in (1, 3, 2):
            at = (z + 4 - d) % 4
            await_at(r.datt2.at[p, at], r.datt_s.at[p, d], r.datt_r.at[p, d], on_patch(at, x))

    def prepare(c, half):
        factor = r.m[c, half].reshape(QUERIES, PAIR)
        grads = r.datt2[half].reshape(QUERIES, PAIR).astype(F32)
        scaled = grads * factor
        r.do_t[c, half] = scaled.T.astype(BF16)
        dots = scaled * r.att2[half].reshape(QUERIES, PAIR).astype(F32)
        sums = []
        for h in range(2):
            r.do_m[c, half, h] = of_head(h, scaled).astype(BF16)
            sums.append(jnp.sum(of_head(h, dots), axis=1, keepdims=True))
        r.dots[c, half] = jnp.where(first_head(QUERIES), sums[0], sums[1])

    def backward_part(c, keys_half):
        xc = (x + OFFSETS[c]) % 4
        places = pl.ds(keys_half * QUERIES, QUERIES)

        def block(half, carry):
            if keys_half == 0:
                prepare(c, half)
            keys = r.kv[xc, keys_half, :, 0].reshape(QUERIES, PAIR)
            values = r.kv[xc, keys_half, :, 1].reshape(QUERIES, PAIR)
            found = []
            for h in range(2):
                rows = pl.ds(h * HEAD, HEAD)
                expo = r.expo[c, h, half, :, :, places].reshape(QUERIES, QUERIES)
                prob_grad = matmul_t(r.do_m[c, half, h], values)
                row_dot = r.dots[c, half, :, h * HEAD : h * HEAD + 1]
                score_grad = (expo.astype(F32) * (prob_grad - row_dot)).astype(BF16)
                found.append(matmul(score_grad, keys))
                r.dk[rows] += matmul(r.q_t[half, rows], score_grad)
                r.dv[rows] += matmul(r.do_t[c, half, rows], expo)
            r.dq[half] += jnp.where(first_head(QUERIES), found[0], found[1])
            return carry

        r.dk[...] = jnp.zeros((PAIR, QUERIES), F32)
        r.dv[...] = jnp.zeros((PAIR, QUERIES), F32)
        if c == 3 and keys_half == 0:
            await_grads(0)
            block(0, 0)
            await_grads(1)
            block(1, 0)
        else:
            lax.fori_loop(0, 2, block, 0)
        return r.dk[...].T.reshape(4, HALF, PAIR), r.dv[...].T.reshape(4, HALF, PAIR)

    def weight_step(number):
        for at, work in ((1, weight_b), (3, weight_c), (4, weight_d), (6, weight_e)):
            if number == at:
                work()

    def backward_keys(i):
        part = r.part.at[i]
        dk, dv = backward_part(3, i)
        part[3, 0], part[3, 1] = dk.astype(BF16), dv.astype(BF16)
        for kind, to in ((0, right), (1, left)):
            send(part.at[3, kind], r.pass_in.at[i, kind], r.pass_s.at[i, kind], r.pass_r.at[i, kind], on_patch(z, to))
        if i:
            return_keys(0)
        for c, kind, origin, to in ((1, 0, left, right), (2, 1, right, left)):
            weight_step(4 * i + c - 1)
            found = list(backward_part(c, i))
            await_at(r.pass_in.at[i, kind], r.pass_s.at[i, kind], r.pass_r.at[i, kind], on_patch(z, origin))
            found[kind] = found[kind] + r.pass_in[i, kind].astype(F32)
            part[c, 0], part[c, 1] = found[0].astype(BF16), found[1].astype(BF16)
            send(part.at[c], r.sum_in.at[i, c - 1], r.sum_s.at[i, c - 1], r.sum_r.at[i, c - 1], on_patch(z, to))
        weight_step(4 * i + 2)
        dk, dv = backward_part(0, i)
        part[0, 0], part[0, 1] = dk.astype(BF16), dv.astype(BF16)
        weight_step(4 * i + 3)

    def return_keys(i):
        await_at(r.sum_in.at[i, 0], r.sum_s.at[i, 0], r.sum_r.at[i, 0], on_patch(z, left))
        await_at(r.sum_in.at[i, 1], r.sum_s.at[i, 1], r.sum_r.at[i, 1], on_patch(z, right))
        for d in (1, 3, 2, 0):
            to = (z + d) % 4
            for kind in range(2):
                total = r.part[i, 0, kind, to].astype(F32)
                total = total + r.sum_in[i, 0, kind, to].astype(F32) + r.sum_in[i, 1, kind, to].astype(F32)
                if d:
                    r.z_out[i, d, kind] = total.astype(BF16)
                else:
                    r.z_in[z, kind, i] = total.astype(BF16)
            if d:
                target = r.z_in.at[z, pl.ds(0, 2), i]
                send(r.z_out.at[i, d], target, r.zkv_s.at[i, d], r.zkv_r.at[i, d], on_patch(to, x))

    backward_keys(0)
    backward_keys(1)
    for half in range(2):
        blocks = (r.dq[half] * SCALE).astype(BF16).reshape(4, HALF, PAIR)
        for to in range(4):
            r.dq_out[to, half] = blocks[to]
    for d in (1, 3, 2):
        to = (z + d) % 4
        send(r.dq_out.at[to], r.z_in.at[z, 2], r.zq_s.at[d], r.zq_r.at[d], on_patch(to, x))
    r.z_in[z, 2] = r.dq_out[z]
    return_keys(1)
    weight_out()
    for d in (1, 3, 2):
        at = (z + 4 - d) % 4
        await_at(r.z_in.at[at, 2], r.zq_s.at[d], r.zq_r.at[d], on_patch(at, x))
        for i in range(2):
            await_at(r.z_in.at[at, pl.ds(0, 2), i], r.zkv_s.at[i, d], r.zkv_r.at[i, d], on_patch(at, x))
    for copy in started:
        copy.wait_send()


def finish(z_in, weight, features, d_queries, d_keys, d_values, d_weight, d_features):
    d_keys[...] = z_in[0, 0].reshape(ROWS, PAIR).astype(F32)
    d_values[...] = z_in[0, 1].reshape(ROWS, PAIR).astype(F32)
    d_queries[...] = z_in[0, 2].reshape(ROWS, PAIR).astype(F32)
    d_weight[...] = weight[...].astype(F32)
    d_features[...] = features[...]


def on_device(patch_queries, patch_keys, patch_values, residual, teacher, output_weight):
    vmem = pl.BlockSpec(memory_space=pltpu.VMEM)
    hbm = pl.BlockSpec(memory_space=pl.ANY)
    z_in, weight, features = pl.pallas_call(
        kernel,
        out_shape=[jax.ShapeDtypeStruct(shape, dtype) for shape, dtype in OUTPUTS.values()],
        in_specs=[hbm] * 6,
        out_specs=[vmem] * 3,
        scratch_shapes=list(SCRATCH.values()),
        compiler_params=pltpu.CompilerParams(
            collective_id=0, has_side_effects=True, vmem_limit_bytes=VMEM_LIMIT
        ),
        cost_estimate=pl.CostEstimate(
            flops=18_000_000_000, bytes_accessed=10_000_000, transcendentals=9_000_000
        ),
    )(
        *(array.reshape(2, HALF, 512) for array in (patch_queries, patch_keys, patch_values)),
        teacher[0],
        residual[0],
        output_weight,
    )
    head_columns = pl.BlockSpec((ROWS, PAIR), lambda i: (0, i))
    d_queries, d_keys, d_values, d_weight, d_features = pl.pallas_call(
        finish,
        grid=(4,),
        out_shape=[jax.ShapeDtypeStruct((ROWS, 512), F32)] * 3
        + [jax.ShapeDtypeStruct((512, D), F32), jax.ShapeDtypeStruct((ROWS, D), F32)],
        in_specs=[
            pl.BlockSpec((1, 3, 2, HALF, PAIR), lambda i: (i, 0, 0, 0, 0)),
            pl.BlockSpec((PAIR, D), lambda i: (i, 0)),
            pl.BlockSpec((64, D), lambda i: (i, 0)),
        ],
        out_specs=[head_columns] * 3
        + [pl.BlockSpec((PAIR, D), lambda i: (i, 0)), pl.BlockSpec((64, D), lambda i: (i, 0))],
        compiler_params=pltpu.CompilerParams(vmem_limit_bytes=VMEM_LIMIT),
    )(z_in, weight.reshape(512, D), features)
    return d_queries[None], d_keys[None], d_values[None], d_features[None], d_weight


def solution(mesh):
    placed = P("dp", "patch", None)
    return jax.shard_map(
        on_device,
        mesh=mesh,
        in_specs=(placed,) * 5 + (P(),),
        out_specs=(placed,) * 4 + (P(),),
        check_vma=False,
    )
```

time: 174 us -> 185 us (1.063); the launches traced: 171 us -> 185 us
  Pallas kernels: 170 us -> 184 us
    pallas_call x1, Pallas kernels: 166 us -> 180 us  [on_device(): pl.pallas_call(kernel, out_shape=[jax.ShapeDtypeStruct(shape, dtype) for...]
where the time goes in v3:
time: 185 us
  Pallas kernels  184 us (99%)
    pallas_call x1, Pallas kernels, on_device(): pl.pallas_call(kernel, out_shape=[jax.ShapeDtypeStruct(shape, dtype) for...  180 us
    pallas_call x1, Pallas kernels, on_device(): pl.pallas_call(finish, grid=(4,), out_shape=[jax.ShapeDtypeStruct((ROWS,...  4.47 us

profile of v3, /device:TPU:2, one launch (start us, length us, event | category | flops | bytes accessed | tf_op | source)
XLA Modules:
  0.0 185.0 jit_solution(11308159807457383234)
XLA Ops:
  0.6 179.8 %shard_map.101 = (bf16[4,3,2,128,128]{4,3,2,1,0:T(8,128)(2,1)}, bf16[8,4,16,1024]{3,2,1,0:T(8,128)(2,1)}, f32[256,1024]{1,0:T(8,128)}) custom-call(bf16[2,128,512]{2,1,0:T(8,128)(2,1)} %bitcast.17, bf16[2,128,512]{2,1,0:T(8,128)(2,1)} %bitcast.18, bf16[2,128,512]{2,1,0:T(8,128)(2,1)} %bitcast.19, bf16[256,1024]{1,0:T(8,128)(2,1)} %bitcast.13, ...), custom_call_target="tpu_custom_call" | custom-call | flops 17999998976 | bytes 10000000 | tf_op jit(solution)/shard_map/pallas_call | solution.py:572
  180.4 4.5 %shard_map.102 = (f32[256,512]{1,0:T(8,128)}, f32[256,512]{1,0:T(8,128)}, f32[256,512]{1,0:T(8,128)}, f32[512,1024]{1,0:T(8,128)}, f32[256,1024]{1,0:T(8,128)}) custom-call(bf16[4,3,2,128,128]{4,3,2,1,0:T(8,128)(2,1)} %get-tuple-element.13.z_in, bf16[512,1024]{1,0:T(8,128)(2,1)} %bitcast.10, f32[256,1024]{1,0:T(8,128)} %get-tuple-element.15.features), custom_call_target="tpu_custom_call" | custom-call | tf_op jit(solution)/shard_map/pallas_call | solution.py:591

commit v4 on v2

--- a/solution.py
+++ b/solution.py
@@ -33,7 +33,7 @@
 
 OUTPUTS = {
     "z_in": ((4, 3, ROWS, PAIR), BF16),
-    "ge": ((8, 4, 16, D), BF16),
+    "ge": ((2, 4, 4, 16, D), BF16),
     "d_features": ((ROWS, D), F32),
 }
 SCRATCH = {
@@ -53,6 +53,13 @@
     "spread_s": dma(2, 4), "spread_r": dma(2, 4),
     "relay_s": dma(2, 4), "relay_r": dma(2, 4),
     "att_s": dma(4), "att_r": dma(4), "att_own": dma(1),
+    "far_kv": on_chip(2, ROWS, PAIR),
+    "far_q": on_chip(2, HALF, PAIR),
+    "far_att": on_chip(2, HALF, PAIR),
+    "far_datt": on_chip(2, HALF, PAIR),
+    "far_dkv": on_chip(2, ROWS, PAIR),
+    "far_dq": on_chip(2, HALF, PAIR),
+    "first_s": dma(6, 2), "first_r": dma(6, 2), "second_s": dma(6, 2), "second_r": dma(6, 2),
     "t_row": on_chip(4, ROWS, D),
     "t_sh": on_chip(ROWS, D),
     "t_ext": on_chip(ROWS, D),
@@ -88,12 +95,13 @@
     "pass_s": dma(2), "pass_r": dma(2), "sum_s": dma(2), "sum_r": dma(2),
     "zkv_s": dma(4), "zkv_r": dma(4), "zq_s": dma(4), "zq_r": dma(4),
     "w_term": on_chip(512, D),
-    "ra": on_chip(7, 64, D), "pa": on_chip(64, D),
+    "rs": on_chip(256, D), "ps": on_chip(256, D),
+    "ra": on_chip(3, 64, D), "pa": on_chip(64, D),
     "rb": on_chip(3, 16, D), "pb": on_chip(16, D),
     "rc": on_chip(8, 16, D), "pc": on_chip(16, D),
     "gd": on_chip(4, 16, D),
-    "wa_s": dma(8), "wa_r": dma(8), "wb_s": dma(4), "wb_r": dma(4), "wc_s": dma(8), "wc_r": dma(8),
-    "wd_s": dma(4), "wd_r": dma(4), "we_s": dma(8), "we_r": dma(8),
+    "ws_s": dma(1), "ws_r": dma(1), "wa_s": dma(4), "wa_r": dma(4), "wb_s": dma(4), "wb_r": dma(4), "wc_s": dma(8), "wc_r": dma(8),
+    "wd_s": dma(4), "wd_r": dma(4), "we_s": dma(4), "we_r": dma(4), "wf_s": dma(1), "wf_r": dma(1),
 }
 INPUTS = ("q", "k", "v", "teacher", "residual", "weight")
 NAMES = INPUTS + tuple(OUTPUTS) + tuple(SCRATCH)
@@ -132,16 +140,19 @@
     z, x = index // 4, index % 4
     dp = lax.axis_index("dp")
     y, z_lo, core = dp // 4, (dp // 2) % 2, dp % 2
-    near, ring = y * 2 + core, z * 2 + z_lo
+    ring = z * 2 + z_lo
     right, left, across = (x + 1) % 4, (x + 3) % 4, (x + 2) % 4
+    up, down, opposite = (z + 1) % 4, (z + 3) % 4, (z + 2) % 4
     high = x // 2
     step = 3 - 2 * high
     shift_to, shift_from = (z + step) % 4, (z + 4 - step) % 4
     swap = x + 1 - 2 * (x % 2)
     inner = (x * (3 - x)) // 2
 
-    def near_device(i):
-        return {"dp": (i // 2) * 4 + z_lo * 2 + i % 2}
+    sibling = {"dp": y * 4 + z_lo * 2 + 1 - core}
+
+    def on_y(i):
+        return {"dp": i * 4 + z_lo * 2 + core}
 
     def ring_device(i):
         return {"dp": y * 4 + (i % 2) * 2 + core, "patch": (i // 2) * 4 + x}
@@ -155,6 +166,21 @@
 
     def await_at(slot, send_sem, recv_sem, device):
         remote(slot, slot, send_sem, recv_sem, device).wait_recv()
+
+    def first_leg(n, relay, by_up, by_down):
+        send(by_up, relay.at[0], r.first_s.at[n, 0], r.first_r.at[n, 0], on_patch(up, x))
+        send(by_down, relay.at[1], r.first_s.at[n, 1], r.first_r.at[n, 1], on_patch(down, x))
+
+    def second_leg(n, relay, to_up, to_down):
+        for i, origin, to, target in ((0, down, up, to_up), (1, up, down, to_down)):
+            await_at(relay.at[i], r.first_s.at[n, i], r.first_r.at[n, i], on_patch(origin, x))
+            send(relay.at[i], target, r.second_s.at[n, i], r.second_r.at[n, i], on_patch(to, x))
+
+    def await_far(n, by_up, by_down):
+        await_at(by_up, r.second_s.at[n, 0], r.second_r.at[n, 0], on_patch(down, x))
+        await_at(by_down, r.second_s.at[n, 1], r.second_r.at[n, 1], on_patch(up, x))
+
+    top, low = pl.ds(0, HALF), pl.ds(HALF, HALF)
 
     local = [
         pltpu.make_async_copy(r.teacher, r.t_raw, r.local.at[0]),
@@ -169,18 +195,21 @@
     peers = (
         [ring_device((ring + d) % 8) for d in range(1, 8)]
         + [on_patch(z, (x + d) % 4) for d in range(1, 4)]
-        + [near_device((near + d) % 8) for d in range(1, 8)]
+        + [on_y((y + d) % 4) for d in range(1, 4)]
+        + [sibling]
     )
     barrier = pltpu.get_barrier_semaphore()
     for peer in peers:
         pl.semaphore_signal(barrier, inc=1, device_id=peer, device_id_type=MESH)
     pl.semaphore_wait(barrier, len(peers))
 
-    for d in (1, 3, 2):
+    first_leg(0, r.far_kv, r.k.at[:, columns(opposite)], r.v.at[:, columns(opposite)])
+    for d in (1, 3):
         to = (z + d) % 4
         for i, source in enumerate((r.k, r.v)):
             send(source.at[:, columns(to)], r.kv.at[x, z, i], r.qkv_s.at[i, d], r.qkv_r.at[i, d], on_patch(to, x))
-    for d in (1, 3, 2):
+    first_leg(1, r.far_q, r.q.at[top, columns(opposite)], r.q.at[low, columns(opposite)])
+    for d in (1, 3):
         to = (z + d) % 4
         send(r.q.at[:, columns(to)], r.q2.at[z], r.qkv_s.at[2, d], r.qkv_r.at[2, d], on_patch(to, x))
 
@@ -200,16 +229,17 @@
     ).astype(BF16)
     for side, to in enumerate((right, left)):
         send(r.t_row.at[x], r.t_row.at[x], r.tx_s.at[side], r.tx_r.at[side], on_patch(z, to))
-    for d in (1, 3, 2):
+    second_leg(0, r.far_kv, r.kv.at[x, down, 0], r.kv.at[x, up, 1])
+    for d in (1, 3):
         at = (z + 4 - d) % 4
         for i in range(2):
             await_at(r.kv.at[x, at, i], r.qkv_s.at[i, d], r.qkv_r.at[i, d], on_patch(at, x))
         spread(d)
+    second_leg(1, r.far_q, r.q2.at[down, top], r.q2.at[up, low])
+    await_far(0, r.kv.at[x, opposite, 0], r.kv.at[x, opposite, 1])
+    spread(2)
     send(r.t_row.at[x], r.t_sh, r.tz_s.at[0], r.tz_r.at[0], on_patch(shift_to, x))
     local[3].wait()
-    for d in (1, 3, 2):
-        at = (z + 4 - d) % 4
-        await_at(r.q2.at[at], r.qkv_s.at[2, d], r.qkv_r.at[2, d], on_patch(at, x))
 
     first_head = lax.broadcasted_iota(jnp.int32, (ROWS, PAIR), 1) < HEAD
 
@@ -252,7 +282,23 @@
         for c in range(4):
             r.m[c, qt] = scale[c] * inverse
 
-    forward_chunk(0)
+    def first_block(i, carry):
+        d = i + (i // 2) * (1 - 2 * (i % 2))
+        for near in (1, 3):
+
+            @pl.when(d == near)
+            def _():
+                at = (z + 4 - near) % 4
+                await_at(r.q2.at[at], r.qkv_s.at[2, near], r.qkv_r.at[2, near], on_patch(at, x))
+
+        @pl.when(d == 2)
+        def _():
+            await_far(1, r.q2.at[opposite, top], r.q2.at[opposite, low])
+
+        forward_block(0, (z + 4 - d) % 4)
+        return carry
+
+    lax.fori_loop(0, 4, first_block, 0)
     for d in (0, 1, 3, 2):
         at = (z + 4 - d) % 4
         await_at(r.kv.at[right, at], r.spread_s.at[1, d], r.spread_r.at[1, d], on_patch(z, right))
@@ -281,21 +327,25 @@
         at = (z + 4 - d) % 4
         for i in range(2):
             await_at(r.kv.at[across, at, i], r.relay_s.at[i, d], r.relay_r.at[i, d], on_patch(z, right))
-    for d in (1, 3, 2, 0):
+    for d in (2, 1, 3, 0):
         to = (z + d) % 4
         forward_block(3, to)
         join(to)
-        if d:
+        if d == 2:
+            first_leg(2, r.far_att, r.att2.at[to, top], r.att2.at[to, low])
+        elif d:
             send(r.att2.at[to], r.att_full.at[:, columns(z)], r.att_s.at[d], r.att_r.at[d], on_patch(to, x))
     own = pltpu.make_async_copy(r.att2.at[z], r.att_full.at[:, columns(z)], r.att_own.at[0])
     own.start()
+    second_leg(2, r.far_att, r.att_full.at[top, columns(down)], r.att_full.at[low, columns(up)])
 
     await_at(r.t_sh, r.tz_s.at[0], r.tz_r.at[0], on_patch(shift_from, x))
     send(r.t_sh, r.t_ext, r.te_s.at[0], r.te_r.at[0], on_patch(z, swap))
     own.wait()
     local[4].wait()
     local[5].wait()
-    for d in (1, 3, 2):
+    await_far(2, r.att_full.at[top, columns(opposite)], r.att_full.at[low, columns(opposite)])
+    for d in (1, 3):
         at = (z + 4 - d) % 4
         await_at(r.att_full.at[:, columns(at)], r.att_s.at[d], r.att_r.at[d], on_patch(at, x))
 
@@ -351,26 +401,37 @@
         rounded = grad.astype(BF16)
         r.grad[rows] = rounded
         r.datt[rows] = matmul_t(rounded, r.w[...]).astype(BF16)
-        for d in (1, 3, 2):
+        side = (up, down)[p]
+        source = r.datt.at[rows, columns(opposite)]
+        send(source, r.far_datt.at[p], r.first_s.at[3, p], r.first_r.at[3, p], on_patch(side, x))
+        for d in (1, 3):
             to = (z + d) % 4
             source = r.datt.at[rows, columns(to)]
             send(source, r.datt2.at[z, rows], r.datt_s.at[p, d], r.datt_r.at[p, d], on_patch(to, x))
         own = pltpu.make_async_copy(r.datt.at[rows, columns(z)], r.datt2.at[z, rows], r.datt_own.at[p])
         own.start()
         datt_own.append(own)
+    second_leg(3, r.far_datt, r.datt2.at[down, top], r.datt2.at[up, low])
     transposed = r.att_full[...].astype(F32).T.astype(BF16)
     r.w_term[...] = matmul(transposed, r.grad[...]).astype(BF16)
 
+    def weight_sibling():
+        rows = pl.ds(pl.multiple_of((1 - core) * 256, 256), 256)
+        send(r.w_term.at[rows], r.rs, r.ws_s.at[0], r.ws_r.at[0], sibling)
+
     def weight_a():
-        for d in range(1, 8):
-            to = (near + d) % 8
+        await_at(r.rs, r.ws_s.at[0], r.ws_r.at[0], sibling)
+        own_rows = pl.ds(pl.multiple_of(core * 256, 256), 256)
+        r.ps[...] = (r.w_term[own_rows].astype(F32) + r.rs[...].astype(F32)).astype(BF16)
+        for d in (2, 1, 3):
+            to = (y + d) % 4
             rows = pl.ds(pl.multiple_of(to * 64, 64), 64)
-            send(r.w_term.at[rows], r.ra.at[d - 1], r.wa_s.at[d], r.wa_r.at[d], near_device(to))
+            send(r.ps.at[rows], r.ra.at[d - 1], r.wa_s.at[d], r.wa_r.at[d], on_y(to))
 
     def weight_b():
-        total = r.w_term[pl.ds(pl.multiple_of(near * 64, 64), 64)].astype(F32)
-        for d in range(1, 8):
-            await_at(r.ra.at[d - 1], r.wa_s.at[d], r.wa_r.at[d], near_device((near + d) % 8))
+        total = r.ps[pl.ds(pl.multiple_of(y * 64, 64), 64)].astype(F32)
+        for d in range(1, 4):
+            await_at(r.ra.at[d - 1], r.wa_s.at[d], r.wa_r.at[d], on_y((y + d) % 4))
             total = total + r.ra[d - 1].astype(F32)
         r.pa[...] = total.astype(BF16)
         for d in range(1, 4):
@@ -404,25 +465,31 @@
         for d in range(1, 4):
             at = (x + 4 - d) % 4
             await_at(r.gd.at[at], r.wd_s.at[d], r.wd_r.at[d], on_patch(z, at))
-        r.ge[near] = r.gd[...]
-        for d in range(1, 8):
-            send(r.gd, r.ge.at[near], r.we_s.at[d], r.we_r.at[d], near_device((near + d) % 8))
+        r.ge[core, y] = r.gd[...]
+        for d in range(1, 4):
+            send(r.gd, r.ge.at[core, y], r.we_s.at[d], r.we_r.at[d], on_y((y + d) % 4))
+
+    def weight_f():
+        for d in range(1, 4):
+            at = (y + 4 - d) % 4
+            await_at(r.ge.at[core, at], r.we_s.at[d], r.we_r.at[d], on_y(at))
+        send(r.ge.at[core], r.ge.at[core], r.wf_s.at[0], r.wf_r.at[0], sibling)
 
     def weight_out():
-        for d in range(1, 8):
-            at = (near + 8 - d) % 8
-            await_at(r.ge.at[at], r.we_s.at[d], r.we_r.at[d], near_device(at))
-
-    weight_a()
+        await_at(r.ge.at[1 - core], r.wf_s.at[0], r.wf_r.at[0], sibling)
+
+    weight_sibling()
     for qt in range(4):
         r.q_t[qt] = (r.q2[qt].astype(F32) * SCALE).T.astype(BF16)
         r.dq[qt] = jnp.zeros((ROWS, PAIR), F32)
-    for p in range(PIECES):
+    weight_a()
+    for p in range(2):
         datt_own[p].wait()
-        for d in (1, 3, 2):
+        for d in (1, 3):
             at = (z + 4 - d) % 4
             slot = r.datt2.at[at, pl.ds(p * PIECE, PIECE)]
             await_at(slot, r.datt_s.at[p, d], r.datt_r.at[p, d], on_patch(at, x))
+    await_far(3, r.datt2.at[opposite, top], r.datt2.at[opposite, low])
 
     def backward_chunk(c):
         xc = (x + OFFSETS[c]) % 4
@@ -473,17 +540,17 @@
     weight_d()
     dk, dv = backward_chunk(0)
     r.part[0, 0], r.part[0, 1] = dk.astype(BF16), dv.astype(BF16)
-    for d in (1, 3, 2, 0):
+    for to in range(4):
+        r.dq_out[to] = (r.dq[to] * SCALE).astype(BF16)
+    first_leg(5, r.far_dq, r.dq_out.at[opposite, top], r.dq_out.at[opposite, low])
+    for d in (1, 3):
         to = (z + d) % 4
-        r.dq_out[to] = (r.dq[to] * SCALE).astype(BF16)
-        if d:
-            send(r.dq_out.at[to], r.z_in.at[z, 2], r.zq_s.at[d], r.zq_r.at[d], on_patch(to, x))
-        else:
-            r.z_in[z, 2] = r.dq_out[z]
+        send(r.dq_out.at[to], r.z_in.at[z, 2], r.zq_s.at[d], r.zq_r.at[d], on_patch(to, x))
+    r.z_in[z, 2] = r.dq_out[z]
     weight_e()
     await_at(r.sum_in.at[0], r.sum_s.at[0], r.sum_r.at[0], on_patch(z, left))
     await_at(r.sum_in.at[1], r.sum_s.at[1], r.sum_r.at[1], on_patch(z, right))
-    for d in (1, 3, 2, 0):
+    for d in (2, 1, 3, 0):
         to = (z + d) % 4
         for i in range(2):
             total = r.part[0, i, to].astype(F32)
@@ -492,13 +559,20 @@
                 r.z_out[d, i] = total.astype(BF16)
             else:
                 r.z_in[z, i] = total.astype(BF16)
-        if d:
+        if d == 2:
+            first_leg(4, r.far_dkv, r.z_out.at[d, 0], r.z_out.at[d, 1])
+        elif d:
             send(r.z_out.at[d], r.z_in.at[z, pl.ds(0, 2)], r.zkv_s.at[d], r.zkv_r.at[d], on_patch(to, x))
-    weight_out()
-    for d in (1, 3, 2):
+    second_leg(5, r.far_dq, r.z_in.at[down, 2, top], r.z_in.at[up, 2, low])
+    second_leg(4, r.far_dkv, r.z_in.at[down, 0], r.z_in.at[up, 1])
+    weight_f()
+    for d in (1, 3):
         at = (z + 4 - d) % 4
         await_at(r.z_in.at[at, 2], r.zq_s.at[d], r.zq_r.at[d], on_patch(at, x))
         await_at(r.z_in.at[at, pl.ds(0, 2)], r.zkv_s.at[d], r.zkv_r.at[d], on_patch(at, x))
+    await_far(5, r.z_in.at[opposite, 2, top], r.z_in.at[opposite, 2, low])
+    await_far(4, r.z_in.at[opposite, 0], r.z_in.at[opposite, 1])
+    weight_out()
     for copy in started:
         copy.wait_send()
 
@@ -540,6 +614,7 @@
         ],
         out_specs=[head_columns] * 3
         + [pl.BlockSpec((PAIR, D), lambda i: (i, 0)), pl.BlockSpec((64, D), lambda i: (i, 0))],
+        compiler_params=pltpu.CompilerParams(vmem_limit_bytes=VMEM_LIMIT),
     )(z_in, weight.reshape(512, D), features)
     return d_queries[None], d_keys[None], d_values[None], d_features[None], d_weight
 

time: 174 us -> 174 us (level)
  Pallas kernels: 170 us -> 172 us
where the time goes in v4:
time: 174 us; the launch traced here: 172 us
  Pallas kernels  172 us (99%)
    pallas_call x1, Pallas kernels, on_device(): pl.pallas_call(kernel, out_shape=[jax.ShapeDtypeStruct(shape, dtype) for...  167 us
    pallas_call x1, Pallas kernels, on_device(): pl.pallas_call(finish, grid=(4,), out_shape=[jax.ShapeDtypeStruct((ROWS,...  4.47 us

profile of v4, /device:TPU:2, one launch (start us, length us, event | category | flops | bytes accessed | tf_op | source)
XLA Modules:
  0.0 172.2 jit_solution(7444127443345577367)
XLA Ops:
  0.6 167.1 %shard_map.101 = (bf16[4,3,256,128]{3,2,1,0:T(8,128)(2,1)}, bf16[2,4,4,16,1024]{4,3,2,1,0:T(8,128)(2,1)}, f32[256,1024]{1,0:T(8,128)}) custom-call(bf16[256,512]{1,0:T(8,128)(2,1)} %bitcast.17, bf16[256,512]{1,0:T(8,128)(2,1)} %bitcast.18, bf16[256,512]{1,0:T(8,128)(2,1)} %bitcast.19, bf16[256,1024]{1,0:T(8,128)(2,1)} %bitcast.13, f32[256,1024]{1,0:T(8,128)} %bitcast.11, ...), custom_call_target="tpu_custom_call" | custom-call | flops 17999998976 | bytes 10000000 | tf_op jit(solution)/shard_map/pallas_call | solution.py:591
  167.7 4.5 %shard_map.102 = (f32[256,512]{1,0:T(8,128)}, f32[256,512]{1,0:T(8,128)}, f32[256,512]{1,0:T(8,128)}, f32[512,1024]{1,0:T(8,128)}, f32[256,1024]{1,0:T(8,128)}) custom-call(bf16[4,3,256,128]{3,2,1,0:T(8,128)(2,1)} %get-tuple-element.13.z_in, bf16[512,1024]{1,0:T(8,128)(2,1)} %bitcast.10, f32[256,1024]{1,0:T(8,128)} %get-tuple-element.15.features), custom_call_target="tpu_custom_call" | custom-call | tf_op jit(solution)/shard_map/pallas_call | solution.py:605

commit v5 on v4

--- a/solution.py
+++ b/solution.py
@@ -19,7 +19,6 @@
 PIECES = 2
 PIECE = ROWS // PIECES
 SCALE = HEAD ** -0.5
-OFFSETS = (0, 1, 3, 2)
 VMEM_LIMIT = 60 * 1024 * 1024
 
 
@@ -61,18 +60,17 @@
     "far_dq": on_chip(2, HALF, PAIR),
     "first_s": dma(6, 2), "first_r": dma(6, 2), "second_s": dma(6, 2), "second_r": dma(6, 2),
     "t_row": on_chip(4, ROWS, D),
-    "t_sh": on_chip(ROWS, D),
+    "t_lhs": on_chip(2, ROWS, D),
     "t_ext": on_chip(ROWS, D),
-    "tile_own": on_chip(ROWS, KEYS, dtype=F32),
-    "tile_sh": on_chip(ROWS, KEYS, dtype=F32),
+    "tiles": on_chip(4, PIECE, KEYS, dtype=F32),
     "s_row": on_chip(4, ROWS, D),
-    "s_sh": on_chip(PIECES, PIECE, D),
+    "s_lhs": on_chip(4, PIECE, D),
+    "terms": on_chip(4, PIECE, D, dtype=F32),
     "s_ext": on_chip(PIECES, PIECE, D),
     "back_out": on_chip(PIECES, PIECE, D),
     "back_in": on_chip(PIECES, PIECE, D),
     "student": on_chip(ROWS, D, dtype=F32),
     "inverse": on_chip(ROWS, PAIR, dtype=F32),
-    "gradient": on_chip(ROWS, D, dtype=F32),
     "grad": on_chip(ROWS, D),
     "datt": on_chip(ROWS, 512),
     "datt2": on_chip(4, ROWS, PAIR),
@@ -85,6 +83,7 @@
     "q_t": on_chip(4, PAIR, ROWS),
     "do_t": on_chip(PAIR, ROWS),
     "dq": on_chip(4, ROWS, PAIR, dtype=F32),
+    "dots": on_chip(4, ROWS, PAIR, dtype=F32),
     "dk": on_chip(PAIR, KEYS, dtype=F32),
     "dv": on_chip(PAIR, KEYS, dtype=F32),
     "part": on_chip(4, 2, 4, ROWS, PAIR),
@@ -126,6 +125,10 @@
     return pl.ds(pl.multiple_of(index * PAIR, PAIR), PAIR)
 
 
+def around(i):
+    return i + (i // 2) * (1 - 2 * (i % 2))
+
+
 def matmul(a, b):
     return jnp.dot(a, b, preferred_element_type=F32)
 
@@ -163,6 +166,15 @@
         copy = remote(src, dst, send_sem, recv_sem, device)
         copy.start()
         started.append(copy)
+
+    later = []
+
+    def begin(*copy):
+        remote(*copy).start()
+
+    def group(copies):
+        later.append(copies)
+        return copies
 
     def await_at(slot, send_sem, recv_sem, device):
         remote(slot, slot, send_sem, recv_sem, device).wait_recv()
@@ -224,9 +236,9 @@
     spread(0)
     local[0].wait()
     teacher = r.t_raw[...].astype(F32)
-    r.t_row[x] = (
-        teacher * lax.rsqrt(jnp.sum(teacher * teacher, axis=1, keepdims=True) + 1e-06)
-    ).astype(BF16)
+    teacher = teacher * lax.rsqrt(jnp.sum(teacher * teacher, axis=1, keepdims=True) + 1e-06)
+    r.t_row[x] = teacher.astype(BF16)
+    r.t_lhs[1] = teacher.astype(BF16)
     for side, to in enumerate((right, left)):
         send(r.t_row.at[x], r.t_row.at[x], r.tx_s.at[side], r.tx_r.at[side], on_patch(z, to))
     second_leg(0, r.far_kv, r.kv.at[x, down, 0], r.kv.at[x, up, 1])
@@ -238,13 +250,13 @@
     second_leg(1, r.far_q, r.q2.at[down, top], r.q2.at[up, low])
     await_far(0, r.kv.at[x, opposite, 0], r.kv.at[x, opposite, 1])
     spread(2)
-    send(r.t_row.at[x], r.t_sh, r.tz_s.at[0], r.tz_r.at[0], on_patch(shift_to, x))
+    send(r.t_row.at[x], r.t_lhs.at[0], r.tz_s.at[0], r.tz_r.at[0], on_patch(shift_to, x))
     local[3].wait()
 
     first_head = lax.broadcasted_iota(jnp.int32, (ROWS, PAIR), 1) < HEAD
 
     def forward_block(c, qt):
-        xc = (x + OFFSETS[c]) % 4
+        xc = (x + around(c)) % 4
         keys = r.kv[xc, :, 0].reshape(KEYS, PAIR)
         values = r.kv[xc, :, 1].reshape(KEYS, PAIR)
         queries = r.q2[qt].astype(F32) * SCALE
@@ -264,13 +276,6 @@
         r.l[c, qt] = jnp.where(first_head, l0, l1)
         r.o[c, qt] = jnp.where(first_head, o0, o1)
 
-    def forward_chunk(c):
-        def block(qt, carry):
-            forward_block(c, qt)
-            return carry
-
-        lax.fori_loop(0, 4, block, 0)
-
     def join(qt):
         tops = [r.m[c, qt] for c in range(4)]
         top = jnp.maximum(jnp.maximum(tops[0], tops[1]), jnp.maximum(tops[2], tops[3]))
@@ -282,65 +287,91 @@
         for c in range(4):
             r.m[c, qt] = scale[c] * inverse
 
-    def first_block(i, carry):
-        d = i + (i // 2) * (1 - 2 * (i % 2))
-        for near in (1, 3):
-
-            @pl.when(d == near)
-            def _():
-                at = (z + 4 - near) % 4
-                await_at(r.q2.at[at], r.qkv_s.at[2, near], r.qkv_r.at[2, near], on_patch(at, x))
-
-        @pl.when(d == 2)
-        def _():
-            await_far(1, r.q2.at[opposite, top], r.q2.at[opposite, low])
-
-        forward_block(0, (z + 4 - d) % 4)
-        return carry
-
-    lax.fori_loop(0, 4, first_block, 0)
-    for d in (0, 1, 3, 2):
+    def await_queries(d):
         at = (z + 4 - d) % 4
-        await_at(r.kv.at[right, at], r.spread_s.at[1, d], r.spread_r.at[1, d], on_patch(z, right))
-        slot = r.kv.at[right, at, 0]
-        send(slot, slot, r.relay_s.at[0, d], r.relay_r.at[0, d], on_patch(z, left))
-        await_at(r.kv.at[left, at], r.spread_s.at[0, d], r.spread_r.at[0, d], on_patch(z, left))
-        slot = r.kv.at[left, at, 1]
-        send(slot, slot, r.relay_s.at[1, d], r.relay_r.at[1, d], on_patch(z, right))
-    forward_chunk(1)
-
-    def pass_on(row, x_s, x_r, on_s, on_r):
-        await_at(row.at[right], x_s.at[1], x_r.at[1], on_patch(z, right))
-        slot = row.at[right, pl.ds(0, HALF)]
-        send(slot, slot, on_s.at[0], on_r.at[0], on_patch(z, left))
-        await_at(row.at[left], x_s.at[0], x_r.at[0], on_patch(z, left))
-        slot = row.at[left, pl.ds(HALF, HALF)]
-        send(slot, slot, on_s.at[1], on_r.at[1], on_patch(z, right))
+        if d == 2:
+            await_far(1, r.q2.at[at, top], r.q2.at[at, low])
+        elif d:
+            await_at(r.q2.at[at], r.qkv_s.at[2, d], r.qkv_r.at[2, d], on_patch(at, x))
+
+    @group
+    def relay_keys(act):
+        for d in (0, 1, 3, 2):
+            at = (z + 4 - d) % 4
+            if act is begin:
+                await_at(r.kv.at[right, at], r.spread_s.at[1, d], r.spread_r.at[1, d], on_patch(z, right))
+            slot = r.kv.at[right, at, 0]
+            act(slot, slot, r.relay_s.at[0, d], r.relay_r.at[0, d], on_patch(z, left))
+            if act is begin:
+                await_at(r.kv.at[left, at], r.spread_s.at[0, d], r.spread_r.at[0, d], on_patch(z, left))
+            slot = r.kv.at[left, at, 1]
+            act(slot, slot, r.relay_s.at[1, d], r.relay_r.at[1, d], on_patch(z, right))
+
+    def pass_on(act, row, x_s, x_r, on_s, on_r):
+        if act is begin:
+            await_at(row.at[right], x_s.at[1], x_r.at[1], on_patch(z, right))
+        slot = row.at[right, top]
+        act(slot, slot, on_s.at[0], on_r.at[0], on_patch(z, left))
+        if act is begin:
+            await_at(row.at[left], x_s.at[0], x_r.at[0], on_patch(z, left))
+        slot = row.at[left, low]
+        act(slot, slot, on_s.at[1], on_r.at[1], on_patch(z, right))
 
     def await_across(row, on_s, on_r):
         for i in range(2):
             await_at(row.at[across, pl.ds(i * HALF, HALF)], on_s.at[i], on_r.at[i], on_patch(z, right))
 
-    pass_on(r.t_row, r.tx_s, r.tx_r, r.tr_s, r.tr_r)
-    forward_chunk(2)
-    for d in range(4):
-        at = (z + 4 - d) % 4
-        for i in range(2):
-            await_at(r.kv.at[across, at, i], r.relay_s.at[i, d], r.relay_r.at[i, d], on_patch(z, right))
-    for d in (2, 1, 3, 0):
-        to = (z + d) % 4
-        forward_block(3, to)
-        join(to)
-        if d == 2:
-            first_leg(2, r.far_att, r.att2.at[to, top], r.att2.at[to, low])
-        elif d:
-            send(r.att2.at[to], r.att_full.at[:, columns(z)], r.att_s.at[d], r.att_r.at[d], on_patch(to, x))
+    @group
+    def pass_teachers(act):
+        pass_on(act, r.t_row, r.tx_s, r.tx_r, r.tr_s, r.tr_r)
+
+    def await_keys():
+        for d in range(4):
+            at = (z + 4 - d) % 4
+            for i in range(2):
+                await_at(r.kv.at[across, at, i], r.relay_s.at[i, d], r.relay_r.at[i, d], on_patch(z, right))
+
+    @group
+    def send_attended(act, places=(1, 3, 2)):
+        for d in places:
+            to = (z + d) % 4
+            if d == 2:
+                for i, rows, side in ((0, top, up), (1, low, down)):
+                    target = r.far_att.at[i]
+                    act(r.att2.at[to, rows], target, r.first_s.at[2, i], r.first_r.at[2, i], on_patch(side, x))
+            else:
+                act(r.att2.at[to], r.att_full.at[:, columns(z)], r.att_s.at[d], r.att_r.at[d], on_patch(to, x))
+
+    def forward_step(step, carry):
+        c, i = step // 4, step % 4
+        start = (3 - c) // 3
+        qt = (z + start * (4 - around(i)) + (1 - start) * around(3 - i)) % 4
+        for at, work in (
+            (1, lambda: await_queries(1)),
+            (2, lambda: await_queries(3)),
+            (3, lambda: await_queries(2)),
+            (4, lambda: relay_keys(begin)),
+            (8, lambda: pass_teachers(begin)),
+            (12, await_keys),
+        ):
+            pl.when(step == at)(work)
+        forward_block(c, qt)
+
+        @pl.when(c == 3)
+        def _():
+            join(qt)
+
+        for i, d in enumerate((2, 3, 1)):
+            pl.when(step == 12 + i)(lambda d=d: send_attended(begin, (d,)))
+        return carry
+
+    lax.fori_loop(0, 16, forward_step, 0)
     own = pltpu.make_async_copy(r.att2.at[z], r.att_full.at[:, columns(z)], r.att_own.at[0])
     own.start()
     second_leg(2, r.far_att, r.att_full.at[top, columns(down)], r.att_full.at[low, columns(up)])
 
-    await_at(r.t_sh, r.tz_s.at[0], r.tz_r.at[0], on_patch(shift_from, x))
-    send(r.t_sh, r.t_ext, r.te_s.at[0], r.te_r.at[0], on_patch(z, swap))
+    await_at(r.t_lhs.at[0], r.tz_s.at[0], r.tz_r.at[0], on_patch(shift_from, x))
+    send(r.t_lhs.at[0], r.t_ext, r.te_s.at[0], r.te_r.at[0], on_patch(z, swap))
     own.wait()
     local[4].wait()
     local[5].wait()
@@ -352,48 +383,79 @@
     features = r.res[...] + matmul(r.att_full[...], r.w[...])
     inverse = lax.rsqrt(jnp.sum(features * features, axis=1, keepdims=True) + 1e-06)
     student = features * inverse
-    r.s_row[x] = student.astype(BF16)
+    rounded = student.astype(BF16)
+    r.s_row[x] = rounded
     for p in range(PIECES):
+        r.s_lhs[PIECES + p] = rounded[p * PIECE : (p + 1) * PIECE]
         source = r.s_row.at[x, pl.ds(p * PIECE, PIECE)]
-        send(source, r.s_sh.at[p], r.sz_s.at[p], r.sz_r.at[p], on_patch(shift_to, x))
+        send(source, r.s_lhs.at[p], r.sz_s.at[p], r.sz_r.at[p], on_patch(shift_to, x))
     for side, to in enumerate((right, left)):
         send(r.s_row.at[x], r.s_row.at[x], r.sx_s.at[side], r.sx_r.at[side], on_patch(z, to))
     r.student[...] = student
     r.inverse[...] = jnp.broadcast_to(inverse, (ROWS, PAIR))
 
+    @group
+    def pass_students(act):
+        pass_on(act, r.s_row, r.sx_s, r.sx_r, r.sr_s, r.sr_r)
+
     await_across(r.t_row, r.tr_s, r.tr_r)
-    r.tile_sh[...] = matmul_t(r.t_sh[...], r.t_row[...].reshape(KEYS, D))
-    pass_on(r.s_row, r.sx_s, r.sx_r, r.sr_s, r.sr_r)
-    r.tile_own[...] = matmul_t(r.t_row[x], r.t_row[...].reshape(KEYS, D))
+
+    def teacher_tile(i, carry):
+        pl.when(i == 1)(lambda: pass_students(begin))
+        tile = matmul_t(r.t_lhs[i], r.t_row[...].reshape(KEYS, D))
+        r.tiles[pl.ds(2 * i, 2)] = tile.reshape(2, PIECE, KEYS)
+        return carry
+
+    lax.fori_loop(0, 2, teacher_tile, 0)
     await_across(r.s_row, r.sr_s, r.sr_r)
 
     first = (1 - high) * (x + 1) * ROWS
     last = KEYS - high * (KEYS - x * ROWS)
-    for p in range(PIECES):
-        await_at(r.s_sh.at[p], r.sz_s.at[p], r.sz_r.at[p], on_patch(shift_from, x))
-        send(r.s_sh.at[p], r.s_ext.at[p], r.se_s.at[p], r.se_r.at[p], on_patch(z, swap))
+
+    @group
+    def swap_students(act, pieces=range(PIECES)):
+        for p in pieces:
+            slot = r.s_lhs.at[p]
+            if act is begin:
+                await_at(slot, r.sz_s.at[p], r.sz_r.at[p], on_patch(shift_from, x))
+            act(slot, r.s_ext.at[p], r.se_s.at[p], r.se_r.at[p], on_patch(z, swap))
+
+    @group
+    def send_back(act, pieces=range(PIECES)):
+        for p in pieces:
+            if act is begin:
+                r.back_out[p] = r.terms[p].astype(BF16)
+            act(r.back_out.at[p], r.back_in.at[p], r.back_s.at[p], r.back_r.at[p], on_patch(shift_from, x))
+
+    def term(i, carry):
+        for p in range(PIECES):
+            pl.when(i == p)(lambda p=p: swap_students(begin, (p,)))
         row = r.s_row[...].reshape(KEYS, D)
-        tile = matmul_t(r.s_sh[p], row) - r.tile_sh[pl.ds(p * PIECE, PIECE)]
+        tile = matmul_t(r.s_lhs[i], row) - r.tiles[i]
         at = lax.broadcasted_iota(jnp.int32, tile.shape, 1)
-        tile = jnp.where(jnp.logical_and(at >= first, at < last), tile, 0.0)
-        r.back_out[p] = matmul(tile.astype(BF16), row).astype(BF16)
-        send(r.back_out.at[p], r.back_in.at[p], r.back_s.at[p], r.back_r.at[p], on_patch(shift_from, x))
-    row = r.s_row[...].reshape(KEYS, D)
-    own_tile = matmul_t(r.s_row[x], row) - r.tile_own[...]
-    r.gradient[...] = matmul(own_tile.astype(BF16), row)
+        whole = i // 2
+        keep = jnp.logical_and(at >= first * (1 - whole), at < last + whole * (KEYS - last))
+        r.terms[i] = matmul(jnp.where(keep, tile, 0.0).astype(BF16), row)
+        for p in range(PIECES):
+            pl.when(i == p)(lambda p=p: send_back(begin, (p,)))
+        return carry
+
+    lax.fori_loop(0, 4, term, 0)
     await_at(r.t_ext, r.te_s.at[0], r.te_r.at[0], on_patch(z, swap))
     for p in range(PIECES):
         await_at(r.s_ext.at[p], r.se_s.at[p], r.se_r.at[p], on_patch(z, swap))
     other = r.s_ext[...].reshape(ROWS, D)
     tile = matmul_t(r.s_row[x], other) - matmul_t(r.t_row[x], r.t_ext[...])
     tile = jnp.where(lax.broadcasted_iota(jnp.int32, tile.shape, 1) < inner * ROWS, tile, 0.0)
-    r.gradient[...] += matmul(tile.astype(BF16), other)
+    added = matmul(tile.astype(BF16), other)
+    for p in range(PIECES):
+        r.terms[PIECES + p] += added[p * PIECE : (p + 1) * PIECE]
 
     datt_own = []
     for p in range(PIECES):
         rows = pl.ds(p * PIECE, PIECE)
         await_at(r.back_in.at[p], r.back_s.at[p], r.back_r.at[p], on_patch(shift_to, x))
-        gram_grad = 32.0 * (r.gradient[rows] + r.back_in[p].astype(F32))
+        gram_grad = 32.0 * (r.terms[PIECES + p] + r.back_in[p].astype(F32))
         student = r.student[rows]
         dot = jnp.sum(student * gram_grad, axis=1, keepdims=True)
         grad = r.inverse[rows, :1] * (gram_grad - student * dot)
@@ -428,16 +490,25 @@
             rows = pl.ds(pl.multiple_of(to * 64, 64), 64)
             send(r.ps.at[rows], r.ra.at[d - 1], r.wa_s.at[d], r.wa_r.at[d], on_y(to))
 
+    @group
+    def send_b(act):
+        for d in range(1, 4):
+            to = (x + d) % 4
+            rows = pl.ds(pl.multiple_of(to * 16, 16), 16)
+            act(r.pa.at[rows], r.rb.at[d - 1], r.wb_s.at[d], r.wb_r.at[d], on_patch(z, to))
+
     def weight_b():
         total = r.ps[pl.ds(pl.multiple_of(y * 64, 64), 64)].astype(F32)
         for d in range(1, 4):
             await_at(r.ra.at[d - 1], r.wa_s.at[d], r.wa_r.at[d], on_y((y + d) % 4))
             total = total + r.ra[d - 1].astype(F32)
         r.pa[...] = total.astype(BF16)
-        for d in range(1, 4):
-            to = (x + d) % 4
-            rows = pl.ds(pl.multiple_of(to * 16, 16), 16)
-            send(r.pa.at[rows], r.rb.at[d - 1], r.wb_s.at[d], r.wb_r.at[d], on_patch(z, to))
+        send_b(begin)
+
+    @group
+    def send_c(act):
+        for d in range(1, 8):
+            act(r.pb, r.rc.at[ring], r.wc_s.at[d], r.wc_r.at[d], ring_device((ring + d) % 8))
 
     def weight_c():
         total = r.pa[pl.ds(pl.multiple_of(x * 16, 16), 16)].astype(F32)
@@ -446,8 +517,12 @@
             total = total + r.rb[d - 1].astype(F32)
         r.pb[...] = total.astype(BF16)
         r.rc[ring] = r.pb[...]
-        for d in range(1, 8):
-            send(r.pb, r.rc.at[ring], r.wc_s.at[d], r.wc_r.at[d], ring_device((ring + d) % 8))
+        send_c(begin)
+
+    @group
+    def send_d(act):
+        for d in range(1, 4):
+            act(r.pc, r.gd.at[x], r.wd_s.at[d], r.wd_r.at[d], on_patch(z, (x + d) % 4))
 
     def weight_d():
         for d in range(1, 8):
@@ -458,8 +533,7 @@
             total = total + r.rc[i].astype(F32)
         r.pc[...] = total.astype(BF16)
         r.gd[x] = r.pc[...]
-        for d in range(1, 4):
-            send(r.pc, r.gd.at[x], r.wd_s.at[d], r.wd_r.at[d], on_patch(z, (x + d) % 4))
+        send_d(begin)
 
     def weight_e():
         for d in range(1, 4):
@@ -483,63 +557,99 @@
         r.q_t[qt] = (r.q2[qt].astype(F32) * SCALE).T.astype(BF16)
         r.dq[qt] = jnp.zeros((ROWS, PAIR), F32)
     weight_a()
-    for p in range(2):
-        datt_own[p].wait()
-        for d in (1, 3):
-            at = (z + 4 - d) % 4
-            slot = r.datt2.at[at, pl.ds(p * PIECE, PIECE)]
-            await_at(slot, r.datt_s.at[p, d], r.datt_r.at[p, d], on_patch(at, x))
-    await_far(3, r.datt2.at[opposite, top], r.datt2.at[opposite, low])
-
-    def backward_chunk(c):
-        xc = (x + OFFSETS[c]) % 4
-        r.dk[...] = jnp.zeros((PAIR, KEYS), F32)
-        r.dv[...] = jnp.zeros((PAIR, KEYS), F32)
-
-        def block(qt, carry):
-            keys = r.kv[xc, :, 0].reshape(KEYS, PAIR)
-            values = r.kv[xc, :, 1].reshape(KEYS, PAIR)
-            factor = r.m[c, qt]
-            grads = r.datt2[qt].astype(F32)
-            scaled = grads * factor
-            r.do_t[...] = scaled.T.astype(BF16)
-            dots = grads * r.att2[qt].astype(F32)
-            found = []
-            for h in range(2):
-                mask = first_head if h == 0 else jnp.logical_not(first_head)
-                rows = pl.ds(h * HEAD, HEAD)
-                masked = jnp.where(mask, scaled, 0.0).astype(BF16)
-                row_dot = jnp.sum(jnp.where(mask, dots, 0.0), axis=1, keepdims=True)
-                row_dot = row_dot * factor[:, h * HEAD : h * HEAD + 1]
-                expo = r.expo[c, h, qt]
-                prob_grad = matmul_t(masked, values)
-                score_grad = (expo.astype(F32) * (prob_grad - row_dot)).astype(BF16)
-                found.append(matmul(score_grad, keys))
-                r.dk[rows] += matmul(r.q_t[qt, rows], score_grad)
-                r.dv[rows] += matmul(r.do_t[rows], expo)
-            r.dq[qt] += jnp.where(first_head, found[0], found[1])
-            return carry
-
-        lax.fori_loop(0, 4, block, 0)
-        return r.dk[...].T.reshape(4, ROWS, PAIR), r.dv[...].T.reshape(4, ROWS, PAIR)
-
-    dk, dv = backward_chunk(3)
-    r.part[3, 0], r.part[3, 1] = dk.astype(BF16), dv.astype(BF16)
-    send(r.part.at[3, 0], r.pass_in.at[0], r.pass_s.at[0], r.pass_r.at[0], on_patch(z, right))
-    send(r.part.at[3, 1], r.pass_in.at[1], r.pass_s.at[1], r.pass_r.at[1], on_patch(z, left))
-    weight_b()
-    dk, dv = backward_chunk(1)
-    await_at(r.pass_in.at[0], r.pass_s.at[0], r.pass_r.at[0], on_patch(z, left))
-    r.part[1, 0], r.part[1, 1] = (dk + r.pass_in[0].astype(F32)).astype(BF16), dv.astype(BF16)
-    send(r.part.at[1], r.sum_in.at[0], r.sum_s.at[0], r.sum_r.at[0], on_patch(z, right))
-    weight_c()
-    dk, dv = backward_chunk(2)
-    await_at(r.pass_in.at[1], r.pass_s.at[1], r.pass_r.at[1], on_patch(z, right))
-    r.part[2, 0], r.part[2, 1] = dk.astype(BF16), (dv + r.pass_in[1].astype(F32)).astype(BF16)
-    send(r.part.at[2], r.sum_in.at[1], r.sum_s.at[1], r.sum_r.at[1], on_patch(z, left))
-    weight_d()
-    dk, dv = backward_chunk(0)
-    r.part[0, 0], r.part[0, 1] = dk.astype(BF16), dv.astype(BF16)
+
+    def await_grads(d):
+        at = (z + 4 - d) % 4
+        if d == 2:
+            await_far(3, r.datt2.at[at, top], r.datt2.at[at, low])
+            return
+        for p in range(2):
+            if d:
+                slot = r.datt2.at[at, pl.ds(p * PIECE, PIECE)]
+                await_at(slot, r.datt_s.at[p, d], r.datt_r.at[p, d], on_patch(at, x))
+            else:
+                datt_own[p].wait()
+
+    def backward_block(c, qt):
+        xc = (x + around(c)) % 4
+        keys = r.kv[xc, :, 0].reshape(KEYS, PAIR)
+        values = r.kv[xc, :, 1].reshape(KEYS, PAIR)
+        factor = r.m[c, qt]
+        scaled = r.datt2[qt].astype(F32) * factor
+        r.do_t[...] = scaled.T.astype(BF16)
+        dots = r.dots[qt] * factor
+        found = []
+        for h in range(2):
+            mask = first_head if h == 0 else jnp.logical_not(first_head)
+            rows = pl.ds(h * HEAD, HEAD)
+            masked = jnp.where(mask, scaled, 0.0).astype(BF16)
+            expo = r.expo[c, h, qt]
+            prob_grad = matmul_t(masked, values)
+            prob_grad = prob_grad - dots[:, h * HEAD : h * HEAD + 1]
+            score_grad = (expo.astype(F32) * prob_grad).astype(BF16)
+            found.append(matmul(score_grad, keys))
+            r.dk[rows] += matmul(r.q_t[qt, rows], score_grad)
+            r.dv[rows] += matmul(r.do_t[rows], expo)
+        r.dq[qt] += jnp.where(first_head, found[0], found[1])
+
+    def row_dots(qt):
+        dots = r.datt2[qt].astype(F32) * r.att2[qt].astype(F32)
+        sums = [
+            jnp.sum(jnp.where(mask, dots, 0.0), axis=1, keepdims=True)
+            for mask in (first_head, jnp.logical_not(first_head))
+        ]
+        r.dots[qt] = jnp.where(first_head, sums[0], sums[1])
+
+    @group
+    def send_across(act):
+        act(r.part.at[3, 0], r.pass_in.at[0], r.pass_s.at[0], r.pass_r.at[0], on_patch(z, right))
+        act(r.part.at[3, 1], r.pass_in.at[1], r.pass_s.at[1], r.pass_r.at[1], on_patch(z, left))
+
+    @group
+    def send_sides(act, chunks=(1, 2)):
+        for c in chunks:
+            i, origin, to = ((0, left, right), (1, right, left))[c - 1]
+            if act is begin:
+                await_at(r.pass_in.at[i], r.pass_s.at[i], r.pass_r.at[i], on_patch(z, origin))
+                added = r.part[c, i].astype(F32) + r.pass_in[i].astype(F32)
+                r.part[c, i] = added.astype(BF16)
+            act(r.part.at[c], r.sum_in.at[i], r.sum_s.at[i], r.sum_r.at[i], on_patch(z, to))
+
+    def backward_step(step, carry):
+        k, i = step // 4, step % 4
+        c = k + 3 * ((3 - k) // 3) - 3 * (k // 3)
+        qt = (z + 4 - around(i)) % 4
+        for at, d in ((0, 0), (1, 1), (2, 3), (3, 2)):
+            pl.when(step == at)(lambda d=d: await_grads(d))
+
+        @pl.when(k == 0)
+        def _():
+            row_dots(qt)
+
+        @pl.when(i == 0)
+        def _():
+            r.dk[...] = jnp.zeros((PAIR, KEYS), F32)
+            r.dv[...] = jnp.zeros((PAIR, KEYS), F32)
+
+        backward_block(c, qt)
+
+        @pl.when(i == 3)
+        def _():
+            r.part[c, 0] = r.dk[...].T.astype(BF16).reshape(4, ROWS, PAIR)
+            r.part[c, 1] = r.dv[...].T.astype(BF16).reshape(4, ROWS, PAIR)
+
+        for at, work in (
+            (3, lambda: send_across(begin)),
+            (4, weight_b),
+            (7, lambda: send_sides(begin, (1,))),
+            (8, weight_c),
+            (11, lambda: send_sides(begin, (2,))),
+            (12, weight_d),
+        ):
+            pl.when(step == at)(work)
+        return carry
+
+    lax.fori_loop(0, 16, backward_step, 0)
     for to in range(4):
         r.dq_out[to] = (r.dq[to] * SCALE).astype(BF16)
     first_leg(5, r.far_dq, r.dq_out.at[opposite, top], r.dq_out.at[opposite, low])
@@ -575,6 +685,8 @@
     weight_out()
     for copy in started:
         copy.wait_send()
+    for copies in later:
+        copies(lambda *copy: remote(*copy).wait_send())
 
 
 def finish(z_in, weight, features, d_queries, d_keys, d_values, d_weight, d_features):

time: 174 us -> 175 us (level)
  no operation moved by 1% of the time
where the time goes in v5:
time: 175 us; the launch traced here: 172 us
  Pallas kernels  172 us (98%)
    pallas_call x1, Pallas kernels, on_device(): pl.pallas_call(kernel, out_shape=[jax.ShapeDtypeStruct(shape, dtype) for...  167 us
    pallas_call x1, Pallas kernels, on_device(): pl.pallas_call(finish, grid=(4,), out_shape=[jax.ShapeDtypeStruct((ROWS,...  4.47 us

profile of v5, /device:TPU:2, one launch (start us, length us, event | category | flops | bytes accessed | tf_op | source)
XLA Modules:
  0.0 172.2 jit_solution(3230845894282683892)
XLA Ops:
  0.6 167.1 %shard_map.101 = (bf16[4,3,256,128]{3,2,1,0:T(8,128)(2,1)}, bf16[2,4,4,16,1024]{4,3,2,1,0:T(8,128)(2,1)}, f32[256,1024]{1,0:T(8,128)}) custom-call(bf16[256,512]{1,0:T(8,128)(2,1)} %bitcast.17, bf16[256,512]{1,0:T(8,128)(2,1)} %bitcast.18, bf16[256,512]{1,0:T(8,128)(2,1)} %bitcast.19, bf16[256,1024]{1,0:T(8,128)(2,1)} %bitcast.13, f32[256,1024]{1,0:T(8,128)} %bitcast.11, ...), custom_call_target="tpu_custom_call" | custom-call | flops 17999998976 | bytes 10000000 | tf_op jit(solution)/shard_map/pallas_call | solution.py:703
  167.7 4.5 %shard_map.102 = (f32[256,512]{1,0:T(8,128)}, f32[256,512]{1,0:T(8,128)}, f32[256,512]{1,0:T(8,128)}, f32[512,1024]{1,0:T(8,128)}, f32[256,1024]{1,0:T(8,128)}) custom-call(bf16[4,3,256,128]{3,2,1,0:T(8,128)(2,1)} %get-tuple-element.13.z_in, bf16[512,1024]{1,0:T(8,128)(2,1)} %bitcast.10, f32[256,1024]{1,0:T(8,128)} %get-tuple-element.15.features), custom_call_target="tpu_custom_call" | custom-call | tf_op jit(solution)/shard_map/pallas_call | solution.py:717

commit v6 on v5

--- a/solution.py
+++ b/solution.py
@@ -83,6 +83,7 @@
     "q_t": on_chip(4, PAIR, ROWS),
     "do_t": on_chip(PAIR, ROWS),
     "dq": on_chip(4, ROWS, PAIR, dtype=F32),
+    "v_one": on_chip(2, KEYS, PAIR),
     "dots": on_chip(4, ROWS, PAIR, dtype=F32),
     "dk": on_chip(PAIR, KEYS, dtype=F32),
     "dv": on_chip(PAIR, KEYS, dtype=F32),
@@ -255,26 +256,28 @@
 
     first_head = lax.broadcasted_iota(jnp.int32, (ROWS, PAIR), 1) < HEAD
 
+    def value_ones(c):
+        values = r.kv[(x + around(c)) % 4, :, 1].reshape(KEYS, PAIR).astype(F32)
+        mask = lax.broadcasted_iota(jnp.int32, (KEYS, PAIR), 1) < HEAD
+        r.v_one[0] = jnp.where(mask, values, 1.0).astype(BF16)
+        r.v_one[1] = jnp.where(mask, 1.0, values).astype(BF16)
+
+    def of_head(h, block):
+        return jnp.where(first_head if h == 0 else jnp.logical_not(first_head), block, 0.0).astype(BF16)
+
     def forward_block(c, qt):
-        xc = (x + around(c)) % 4
-        keys = r.kv[xc, :, 0].reshape(KEYS, PAIR)
-        values = r.kv[xc, :, 1].reshape(KEYS, PAIR)
+        keys = r.kv[(x + around(c)) % 4, :, 0].reshape(KEYS, PAIR)
         queries = r.q2[qt].astype(F32) * SCALE
-        parts = []
+        scores = [matmul_t(of_head(h, queries), keys) for h in range(2)]
+        tops, weighted = [], []
         for h in range(2):
-            mask = first_head if h == 0 else jnp.logical_not(first_head)
-            masked = jnp.where(mask, queries, 0.0).astype(BF16)
-            scores = matmul_t(masked, keys)
-            top = jnp.max(scores, axis=1, keepdims=True)
-            expo = jnp.exp(scores - top)
-            total = jnp.sum(expo, axis=1, keepdims=True)
-            rounded = expo.astype(BF16)
+            tops.append(jnp.max(scores[h], axis=1, keepdims=True))
+            rounded = jnp.exp(scores[h] - tops[h]).astype(BF16)
             r.expo[c, h, qt] = rounded
-            parts.append((top, total, matmul(rounded, values)))
-        (m0, l0, o0), (m1, l1, o1) = parts
-        r.m[c, qt] = jnp.where(first_head, m0, m1)
-        r.l[c, qt] = jnp.where(first_head, l0, l1)
-        r.o[c, qt] = jnp.where(first_head, o0, o1)
+            weighted.append(matmul(rounded, r.v_one[h]))
+        r.m[c, qt] = jnp.where(first_head, *tops)
+        r.o[c, qt] = jnp.where(first_head, *weighted)
+        r.l[c, qt] = pltpu.roll(jnp.where(first_head, *weighted[::-1]), HEAD, 1)
 
     def join(qt):
         tops = [r.m[c, qt] for c in range(4)]
@@ -355,6 +358,7 @@
             (12, await_keys),
         ):
             pl.when(step == at)(work)
+        pl.when(i == 0)(lambda: value_ones(c))
         forward_block(c, qt)
 
         @pl.when(c == 3)
@@ -370,8 +374,6 @@
     own.start()
     second_leg(2, r.far_att, r.att_full.at[top, columns(down)], r.att_full.at[low, columns(up)])
 
-    await_at(r.t_lhs.at[0], r.tz_s.at[0], r.tz_r.at[0], on_patch(shift_from, x))
-    send(r.t_lhs.at[0], r.t_ext, r.te_s.at[0], r.te_r.at[0], on_patch(z, swap))
     own.wait()
     local[4].wait()
     local[5].wait()
@@ -398,6 +400,8 @@
     def pass_students(act):
         pass_on(act, r.s_row, r.sx_s, r.sx_r, r.sr_s, r.sr_r)
 
+    await_at(r.t_lhs.at[0], r.tz_s.at[0], r.tz_r.at[0], on_patch(shift_from, x))
+    send(r.t_lhs.at[0], r.t_ext, r.te_s.at[0], r.te_r.at[0], on_patch(z, swap))
     await_across(r.t_row, r.tr_s, r.tr_r)
 
     def teacher_tile(i, carry):
@@ -578,19 +582,18 @@
         scaled = r.datt2[qt].astype(F32) * factor
         r.do_t[...] = scaled.T.astype(BF16)
         dots = r.dots[qt] * factor
-        found = []
+        prob_grads, expos, found = [], [], []
         for h in range(2):
-            mask = first_head if h == 0 else jnp.logical_not(first_head)
+            expos.append(r.expo[c, h, qt])
+            prob_grads.append(matmul_t(of_head(h, scaled), values))
+        for h in range(2):
             rows = pl.ds(h * HEAD, HEAD)
-            masked = jnp.where(mask, scaled, 0.0).astype(BF16)
-            expo = r.expo[c, h, qt]
-            prob_grad = matmul_t(masked, values)
-            prob_grad = prob_grad - dots[:, h * HEAD : h * HEAD + 1]
-            score_grad = (expo.astype(F32) * prob_grad).astype(BF16)
+            r.dv[rows] += matmul(r.do_t[rows], expos[h])
+            prob_grad = prob_grads[h] - dots[:, h * HEAD : h * HEAD + 1]
+            score_grad = expos[h] * prob_grad.astype(BF16)
             found.append(matmul(score_grad, keys))
             r.dk[rows] += matmul(r.q_t[qt, rows], score_grad)
-            r.dv[rows] += matmul(r.do_t[rows], expo)
-        r.dq[qt] += jnp.where(first_head, found[0], found[1])
+        r.dq[qt] += jnp.where(first_head, *found)
 
     def row_dots(qt):
         dots = r.datt2[qt].astype(F32) * r.att2[qt].astype(F32)
@@ -640,11 +643,11 @@
 
         for at, work in (
             (3, lambda: send_across(begin)),
-            (4, weight_b),
+            (5, weight_b),
             (7, lambda: send_sides(begin, (1,))),
-            (8, weight_c),
+            (9, weight_c),
             (11, lambda: send_sides(begin, (2,))),
-            (12, weight_d),
+            (13, weight_d),
         ):
             pl.when(step == at)(work)
         return carry

time: 175 us -> 171 us (0.977)
  Pallas kernels: 172 us -> 168 us
    pallas_call x1, Pallas kernels: 167 us -> 163 us  [on_device(): pl.pallas_call(kernel, out_shape=[jax.ShapeDtypeStruct(shape, dtype) for...]
where the time goes in v6:
time: 171 us; the launch traced here: 169 us
  Pallas kernels  168 us (98%)
    pallas_call x1, Pallas kernels, on_device(): pl.pallas_call(kernel, out_shape=[jax.ShapeDtypeStruct(shape, dtype) for...  163 us
    pallas_call x1, Pallas kernels, on_device(): pl.pallas_call(finish, grid=(4,), out_shape=[jax.ShapeDtypeStruct((ROWS,...  4.47 us

profile of v6, /device:TPU:2, one launch (start us, length us, event | category | flops | bytes accessed | tf_op | source)
XLA Modules:
  0.0 168.5 jit_solution(11715116357187830176)
XLA Ops:
  0.6 163.4 %shard_map.101 = (bf16[4,3,256,128]{3,2,1,0:T(8,128)(2,1)}, bf16[2,4,4,16,1024]{4,3,2,1,0:T(8,128)(2,1)}, f32[256,1024]{1,0:T(8,128)}) custom-call(bf16[256,512]{1,0:T(8,128)(2,1)} %bitcast.17, bf16[256,512]{1,0:T(8,128)(2,1)} %bitcast.18, bf16[256,512]{1,0:T(8,128)(2,1)} %bitcast.19, bf16[256,1024]{1,0:T(8,128)(2,1)} %bitcast.13, f32[256,1024]{1,0:T(8,128)} %bitcast.11, ...), custom_call_target="tpu_custom_call" | custom-call | flops 17999998976 | bytes 10000000 | tf_op jit(solution)/shard_map/pallas_call | solution.py:706
  164.0 4.5 %shard_map.102 = (f32[256,512]{1,0:T(8,128)}, f32[256,512]{1,0:T(8,128)}, f32[256,512]{1,0:T(8,128)}, f32[512,1024]{1,0:T(8,128)}, f32[256,1024]{1,0:T(8,128)}) custom-call(bf16[4,3,256,128]{3,2,1,0:T(8,128)(2,1)} %get-tuple-element.13.z_in, bf16[512,1024]{1,0:T(8,128)(2,1)} %bitcast.10, f32[256,1024]{1,0:T(8,128)} %get-tuple-element.15.features), custom_call_target="tpu_custom_call" | custom-call | tf_op jit(solution)/shard_map/pallas_call | solution.py:720
